TPU v7x, 256 devices: a whole 4x4x8 slice. The times are simulated.
256 devices in a mesh: dp: 4 (over x_lo, core), ctx: 64 (over y, x_hi, z).
Axes of the slice: x: 4 (x_hi: 2, x_lo: 2; x = x_hi * 2 + x_lo), y: 4, z: 8, core: 2. Of those that a mesh axis runs over, the one named last changes fastest.
Arguments:
- queries: bfloat16 [4, 2048, 2048], P('dp', 'ctx'), may hold values from -8 to 8
- keys: bfloat16 [4, 2048, 512], P('dp', 'ctx'), may hold values from -8 to 8
- values: bfloat16 [4, 2048, 512], P('dp', 'ctx'), may hold values from -6 to 6
- out_grad: bfloat16 [4, 2048, 2048], P('dp', 'ctx'), may hold values from -6 to 6
- routed_inputs: bfloat16 [4, 2048, 4096], P('dp', 'ctx'), may hold values from -6 to 6
- router_weight: float32 [4096], replicated, may hold values from -0.09375 to 0.09375
- positions: int32 [4, 2048], P('dp', 'ctx'), may hold values from 0 to 16383, as said below
Outputs:
- query_grad: bfloat16 [4, 2048, 2048], P('dp', 'ctx')
- key_grad: bfloat16 [4, 2048, 512], P('dp', 'ctx')
- value_grad: bfloat16 [4, 2048, 512], P('dp', 'ctx')
- router_grad: float32 [4096], replicated
Inputs may be any that keep to these rules, and one draw needn't show every extreme that they name: `positions`: within each sequence strictly increasing, the first 0 and the last 16383.
All inputs are finite; a program needn't handle non-finite values.
Results may differ from a plain program's by a relative error of at most 0.039.
Values may be sent and summed in bfloat16 or wider, within the bound.
A program may use at most 128 MiB of HBM per device.

v0:
```python
import math

import jax
import jax.numpy as jnp
from jax import lax
from jax.sharding import PartitionSpec as P

HQ = 16
KVH = 4
HD = 128


ROPE_BASE = 500000.0
NEG_LARGE = -1e30


def rope_tables(pair_count):
    frequency = [ROPE_BASE ** (-number / pair_count) for number in range(pair_count)]
    coarse = [256.0 * factor % (2.0 * math.pi) for factor in frequency]
    return (jnp.asarray(frequency, jnp.float32), jnp.asarray(coarse, jnp.float32))


def rotation(positions, head_dim):
    frequency, coarse = rope_tables(head_dim // 2)
    upper_part = (positions // 256).astype(jnp.float32)
    lower_part = (positions % 256).astype(jnp.float32)
    angles = upper_part[:, None] * coarse[None, :] + lower_part[:, None] * frequency[None, :]
    return (jnp.cos(angles)[:, None, :], jnp.sin(angles)[:, None, :])


def turn_forward(vectors, cosine, sine):
    width_half = vectors.shape[-1] // 2
    first_half = vectors[..., :width_half]
    second_half = vectors[..., width_half:]
    return jnp.concatenate(
        [first_half * cosine - second_half * sine, second_half * cosine + first_half * sine],
        axis=-1,
    )


def turn_back(vectors, cosine, sine):
    width_half = vectors.shape[-1] // 2
    first_half = vectors[..., :width_half]
    second_half = vectors[..., width_half:]
    return jnp.concatenate(
        [first_half * cosine + second_half * sine, second_half * cosine - first_half * sine],
        axis=-1,
    )


def unchanged(state):
    return state


def shards(queries, keys, values, out_grad, routed_inputs, router_weight, positions):
    slots = queries.shape[1]
    half_rows = slots // 2
    group_size = HQ // KVH
    score_scale = 1.0 / math.sqrt(HD)
    own_places = positions[0]
    cosine, sine = rotation(own_places, HD)
    key_rot = turn_forward(keys[0].astype(jnp.float32).reshape(slots, KVH, HD), cosine, sine)
    key_rot = key_rot.astype(jnp.bfloat16).reshape(slots, KVH * HD)
    key_all, value_all, place_all = (
        lax.all_gather(key_rot, "ctx", axis=0, tiled=True),
        lax.all_gather(values[0], "ctx", axis=0, tiled=True),
        lax.all_gather(own_places, "ctx", axis=0, tiled=True),
    )
    input_wide = routed_inputs[0].astype(jnp.float32)
    own_gate = jax.nn.sigmoid(jnp.dot(input_wide, router_weight, precision=lax.Precision.HIGHEST))
    query_rows = queries[0]
    upstream_rows = out_grad[0]
    held_cos, held_sin = rotation(own_places, HD)
    query_rot = turn_forward(
        query_rows.astype(jnp.float32).reshape(slots, HQ, HD), held_cos, held_sin
    )
    query_rot = query_rot.astype(jnp.bfloat16).reshape(2, half_rows, KVH, group_size, HD)
    upstream = upstream_rows.astype(jnp.float32).reshape(2, half_rows, KVH, group_size, HD)
    scaled_grad = (own_gate.reshape(2, half_rows)[:, :, None, None, None] * upstream).astype(
        jnp.bfloat16
    )
    place_half = own_places.reshape(2, half_rows)
    query_top = jnp.max(place_half, axis=1)
    total_keys = key_all.shape[0]

    def key_block(start, count):
        key_tile = lax.dynamic_slice_in_dim(key_all, start, count, 0).reshape(count, KVH, HD)
        value_tile = lax.dynamic_slice_in_dim(value_all, start, count, 0).reshape(count, KVH, HD)
        place_tile = lax.dynamic_slice_in_dim(place_all, start, count, 0)
        return (key_tile, value_tile, place_tile)

    def tile_scores(which, key_tile, place_tile):
        scores = (
            jnp.einsum(
                "tkgd,ukd->kgtu", query_rot[which], key_tile, preferred_element_type=jnp.float32
            )
            * score_scale
        )
        allowed = place_half[which][:, None] >= place_tile[None, :]
        return jnp.where(allowed[None, None], scores, -jnp.inf)

    block_rows = math.gcd(total_keys, 512)
    block_count = total_keys // block_rows

    def stats_step(number, carry):
        top_all, mass_all = carry
        key_tile, value_tile, place_tile = key_block(number * block_rows, block_rows)
        new_top = []
        new_mass = []
        for which in range(2):

            def stats_live(state, which=which):
                top_old, mass_old = state
                scores = tile_scores(which, key_tile, place_tile)
                top_new = jnp.maximum(top_old, jnp.max(scores, axis=-1))
                mass_new = mass_old * jnp.exp(top_old - top_new) + jnp.sum(
                    jnp.exp(scores - top_new[..., None]), axis=-1
                )
                return (top_new, mass_new)

            top_one, mass_one = lax.cond(
                place_tile[0] <= query_top[which],
                stats_live,
                unchanged,
                (top_all[which], mass_all[which]),
            )
            new_top.append(top_one)
            new_mass.append(mass_one)
        return (jnp.stack(new_top), jnp.stack(new_mass))

    stat_shape = (2, KVH, group_size, half_rows)
    top_all, mass_all = lax.fori_loop(
        0,
        block_count,
        stats_step,
        (jnp.full(stat_shape, NEG_LARGE, jnp.float32), jnp.zeros(stat_shape, jnp.float32)),
    )
    lse = top_all + jnp.log(mass_all)

    def output_step(number, totals):
        key_tile, value_tile, place_tile = key_block(number * block_rows, block_rows)
        parts = []
        for which in range(2):

            def output_live(total, which=which):
                scores = tile_scores(which, key_tile, place_tile)
                probs = jnp.exp(scores - lse[which][..., None]).astype(jnp.bfloat16)
                return total + jnp.einsum(
                    "kgtu,ukd->tkgd", probs, value_tile, preferred_element_type=jnp.float32
                )

            parts.append(
                lax.cond(place_tile[0] <= query_top[which], output_live, unchanged, totals[which])
            )
        return jnp.stack(parts)

    row_shape = (2, half_rows, KVH, group_size, HD)
    attn = lax.fori_loop(0, block_count, output_step, jnp.zeros(row_shape, jnp.float32))
    router_term = jnp.sum(upstream * attn, axis=(2, 3, 4)).reshape(slots)
    logit_grad = own_gate * (1.0 - own_gate) * router_term
    delta = jnp.transpose(jnp.sum(scaled_grad.astype(jnp.float32) * attn, axis=-1), (0, 2, 3, 1))

    def tile_grads(which, key_tile, value_tile, place_tile):
        scores = tile_scores(which, key_tile, place_tile)
        weights = jnp.exp(scores - lse[which][..., None])
        prob_grad = jnp.einsum(
            "tkgd,ukd->kgtu", scaled_grad[which], value_tile, preferred_element_type=jnp.float32
        )
        score_grad = (weights * (prob_grad - delta[which][..., None]) * score_scale).astype(
            jnp.bfloat16
        )
        return (weights, score_grad)

    def query_step(number, totals):
        key_tile, value_tile, place_tile = key_block(number * block_rows, block_rows)
        parts = []
        for which in range(2):

            def query_live(total, which=which):
                weights, score_grad = tile_grads(which, key_tile, value_tile, place_tile)
                return total + jnp.einsum(
                    "kgtu,ukd->tkgd", score_grad, key_tile, preferred_element_type=jnp.float32
                )

            parts.append(
                lax.cond(place_tile[0] <= query_top[which], query_live, unchanged, totals[which])
            )
        return jnp.stack(parts)

    query_acc = lax.fori_loop(0, block_count, query_step, jnp.zeros(row_shape, jnp.float32))
    query_acc = query_acc.reshape(slots, HQ, HD)
    query_done = (
        turn_back(query_acc, held_cos, held_sin).astype(jnp.bfloat16).reshape(slots, HQ * HD)
    )
    tile_rows = math.gcd(lax.axis_size("ctx") * slots, 512)

    def term_step(number, terms):
        key_tile, value_tile, place_tile = key_block(number * tile_rows, tile_rows)
        key_acc = jnp.zeros((tile_rows, KVH, HD), jnp.float32)
        value_acc = jnp.zeros((tile_rows, KVH, HD), jnp.float32)
        for which in range(2):

            def term_live(state, which=which):
                key_old, value_old = state
                weights, score_grad = tile_grads(which, key_tile, value_tile, place_tile)
                probs = weights.astype(jnp.bfloat16)
                key_new = key_old + jnp.einsum(
                    "kgtu,tkgd->ukd",
                    score_grad,
                    query_rot[which],
                    preferred_element_type=jnp.float32,
                )
                value_new = value_old + jnp.einsum(
                    "kgtu,tkgd->ukd", probs, scaled_grad[which], preferred_element_type=jnp.float32
                )
                return (key_new, value_new)

            key_acc, value_acc = lax.cond(
                place_tile[0] <= query_top[which], term_live, unchanged, (key_acc, value_acc)
            )
        piece = jnp.stack(
            [key_acc.reshape(tile_rows, KVH * HD), value_acc.reshape(tile_rows, KVH * HD)], axis=1
        )
        return lax.dynamic_update_slice_in_dim(terms, piece, number * tile_rows, 0)

    key_sums = lax.psum_scatter(
        lax.fori_loop(
            0,
            lax.axis_size("ctx") * slots // tile_rows,
            term_step,
            jnp.zeros((lax.axis_size("ctx") * slots, 2, KVH * HD), jnp.float32),
        ),
        "ctx",
        scatter_dimension=0,
        tiled=True,
    )
    key_grad = (
        turn_back(key_sums[:, 0].reshape(slots, KVH, HD), cosine, sine)
        .astype(jnp.bfloat16)
        .reshape(slots, KVH * HD)
    )
    value_grad = key_sums[:, 1].astype(jnp.bfloat16)
    router_part = jnp.dot(logit_grad, input_wide, precision=lax.Precision.HIGHEST)
    router_total = lax.psum(router_part, ("dp", "ctx"))
    router_grad = router_total / math.sqrt(lax.axis_size("dp") * lax.axis_size("ctx") * slots)
    return (query_done[None], key_grad[None], value_grad[None], router_grad)


def solution(mesh):
    in_specs = (
        P("dp", "ctx", None),
        P("dp", "ctx", None),
        P("dp", "ctx", None),
        P("dp", "ctx", None),
        P("dp", "ctx", None),
        P(),
        P("dp", "ctx"),
    )
    out_specs = (P("dp", "ctx", None), P("dp", "ctx", None), P("dp", "ctx", None), P())
    return jax.shard_map(shards, mesh=mesh, in_specs=in_specs, out_specs=out_specs, check_vma=False)
```

profile of v0, /device:TPU:2, one launch (start us, length us, event | category | flops | bytes accessed | tf_op | source)
XLA Modules:
  0.0 775.5 jit_solution(12466329011470404495)
XLA Ops:
  16.7 27.9 %all-reduce = s32[2048]{0:T(1024)S(1)} all-reduce(s32[2048]{0:T(1024)S(1)} %get-tuple-element.1576), channel_id=2, replica_groups=mesh['dp'=4,'ctx'=64] {'ctx'}, use_global_device_ids=true, to_apply=%add | all-reduce | flops 2048 | bytes 16384 | tf_op jit(solution)/shard_map/all_gather | solution.py:67
  44.6 88.7 %all-gather.5.cloned.1.call-done = bf16[2048,512]{1,0:T(8,128)(2,1)} async-done(((bf16[32,512]{1,0:T(8,128)(2,1)}), bf16[2048,512]{1,0:T(8,128)(2,1)}) %all-gather.5.cloned.1.call-update) | async-done | bytes 2097168 | tf_op jit(solution)/shard_map/all_gather | solution.py:65
  133.3 4.0 copy.136
  137.3 36.0 %while.54 = (s32[]{:T(128)}, f32[2,4,4,16]{3,2,1,0:T(4,128)S(1)}, f32[2,4,4,16]{3,2,1,0:T(4,128)S(1)}, s32[2048]{0:T(1024)S(1)}, s32[2]{0:T(128)S(1)}, /*index=5...) while((s32[]{:T(128)}, f32[2,4,4,16]{3,2,1,0:T(4,128)S(1)}, ...), condition=%wide.region_10.11_spmd, body=%wide.region_1.10_spmd.sunk | while | flops 68438024 | bytes 4410111 | solution.py:132
  142.2 2.7 conditional.17
  146.9 2.7 conditional.16
  173.3 79.1 %all-gather.7.cloned.1.call-done = bf16[1,2048,512]{2,1,0:T(8,128)(2,1)} async-done(((bf16[1,32,512]{2,1,0:T(8,128)(2,1)}), bf16[1,2048,512]{2,1,0:T(8,128)(2,1)}) %all-gather.7.cloned.1.call-update) | async-done | bytes 2097168 | tf_op jit(solution)/shard_map/all_gather | solution.py:66
  252.4 4.0 copy.137
  256.4 21.3 %while.55 = (s32[]{:T(128)}, f32[2,16,4,4,128]{4,1,3,2,0:T(8,128)S(1)}, s32[2048]{0:T(1024)S(1)}, s32[2]{0:T(128)S(1)}, bf16[2048,512]{0,1:T(8,128)(2,1)}, /*ind...) while((s32[]{:T(128)}, ...), condition=%wide.region_16.17_spmd, body=%wide.region_11.16_spmd.sunk | while | flops 135413760 | bytes 5960423 | solution.py:158
  278.7 4.4 broadcast_in_dim.110.clone
  283.1 63.1 %while.57 = (s32[]{:T(128)}, f32[2048,2,512]{2,0,1:T(8,128)}, s32[2048]{0:T(1024)S(1)}, s32[2]{0:T(128)S(1)}, bf16[2048,512]{0,1:T(8,128)(2,1)}, /*index=5*/bf16...) while((s32[]{:T(128)}, f32[2048,2,512]{2,0,1:T(8,128)}, ...), condition=%wide.region_29.30_spmd, body=%wide.region_24.29_spmd.sunk | while | flops 271597568 | bytes 38956244 | solution.py:227
  283.1 1.3 constant_dynamic-slice_fusion.14
  287.0 6.3 conditional.22
  287.4 1.5 convolution_bitcast_fusion.6
  288.9 1.6 copy.203
  290.5 1.3 convolution_bitcast_fusion.5
  291.8 1.6 copy.204
  294.6 9.1 %conditional.23 = (f32[512,1,512]{0,2,1:T(8,128)S(1)}, f32[512,1,512]{0,2,1:T(8,128)S(1)}) conditional(s32[]{:T(128)} %bitcast.518, (f32[512,4,128]{0,2,1:T(8,128)S(1)}, f32[512,4,128]{0,2,1:T(8,128)S(1)}) %get-tuple-element.1880, (s32[2,16]{1,0:T(2,128)S(1)}, s32[512]{0:T(512)S(1)}, bf16[2,16,4,4,128]{4,1,3,2,0:T(8,128)(2,1)S(1)}, ...), branch_computations={%region_27.27_spmd, %region_28.28_spmd} | conditional | flops 135798784 | bytes 11828460 | solution.py:218
  295.3 1.3 fusion.112
  296.6 1.6 copy.126
  298.2 1.3 fusion.104
  299.5 2.6 copy.127
  302.1 1.6 fusion.105
  303.6 1.5 pad_maximum_fusion.18
  305.1 1.9 copy.222
  307.1 1.5 constant_dynamic-update-slice_fusion.2
  308.7 1.3 constant_dynamic-slice_fusion.14
  312.5 2.3 conditional.22
  316.1 1.5 pad_maximum_fusion.18
  317.6 1.9 copy.222
  319.6 1.5 constant_dynamic-update-slice_fusion.2
  321.2 1.3 constant_dynamic-slice_fusion.14
  325.0 2.3 conditional.22
  328.6 1.5 pad_maximum_fusion.18
  330.1 1.9 copy.222
  332.0 1.5 constant_dynamic-update-slice_fusion.2
  333.6 1.3 constant_dynamic-slice_fusion.14
  337.5 2.3 conditional.22
  341.0 1.5 pad_maximum_fusion.18
  342.5 1.9 copy.222
  344.5 1.6 constant_dynamic-update-slice_fusion.2
  346.8 25.5 %while.56 = (s32[]{:T(128)}, f32[2,16,4,4,128]{4,1,3,2,0:T(8,128)S(1)}, s32[2048]{0:T(1024)}, s32[2]{0:T(128)S(1)}, bf16[2048,512]{0,1:T(8,128)(2,1)}, /*index=5...) while((s32[]{:T(128)}, ...), condition=%wide.region_23.24_spmd, body=%wide.region_18.23_spmd.sunk | while | flops 203309056 | bytes 9257751 | solution.py:190
  346.8 1.3 constant_dynamic-slice_fusion.13
  354.3 1.3 constant_dynamic-slice_fusion.13
  360.3 1.3 constant_dynamic-slice_fusion.13
  374.0 122.2 %psum.7 = f32[4096]{0:T(1024)S(1)} all-reduce(f32[4096]{0:T(1024)S(1)} %bitcast.557), channel_id=1, replica_groups=mesh['dp'=4,'ctx'=64] {'dp','ctx'}, use_global_device_ids=true, to_apply=%region_32.33 | all-reduce | flops 4096 | bytes 32768 | tf_op jit(solution)/shard_map/psum | solution.py:244
  496.8 269.0 %reduce-scatter.2.cloned.1.call-done = f32[32,2,512]{2,0,1:T(8,128)} async-done(((f32[2048,2,512]{2,0,1:T(8,128)}), f32[32,2,512]{2,0,1:T(8,128)}) %reduce-scatter.2.cloned.1.call-update) | async-done | bytes 131088 | tf_op jit(solution)/shard_map/reduce_scatter | solution.py:226
  767.5 1.5 fusion.163
  (330 shorter events, 77.7 us)
Async XLA Ops:
  7.2 8.8 %copy-start = (bf16[1,32,4096]{2,1,0:T(8,128)(2,1)S(1)}, bf16[1,32,4096]{2,1,0:T(8,128)(2,1)}, u32[]{:S(2)}) copy-start(bf16[1,32,4096]{2,1,0:T(8,128)(2,1)} %param.39) | copy-start | bytes 786436
  7.2 8.0 %copy-start.22 = (s32[1,32]{1,0:T(1,128)S(1)}, s32[1,32]{1,0:T(1,128)}, u32[]{:S(2)}) copy-start(s32[1,32]{1,0:T(1,128)} %param.41) | copy-start | bytes 388
  7.2 8.8 %copy-start.23 = (f32[4096]{0:T(1024)S(1)}, f32[4096]{0:T(1024)}, u32[]{:S(2)}) copy-start(f32[4096]{0:T(1024)} %param.40) | copy-start | bytes 49156
  7.2 9.2 %copy-start.16 = (bf16[1,32,2048]{2,1,0:T(8,128)(2,1)S(1)}, bf16[1,32,2048]{2,1,0:T(8,128)(2,1)}, u32[]{:S(2)}) copy-start(bf16[1,32,2048]{2,1,0:T(8,128)(2,1)} %param.38) | copy-start | bytes 393220
  7.2 126.1 %all-gather.5.cloned.1.call-start = ((), (), s32[]{:S(2)}) async-start(), calls=%async_computation.1 | async-start | bytes 2129920 | tf_op jit(solution)/shard_map/all_gather | solution.py:65
  11.6 125.7 %copy-start.9 = (f32[32,64]{1,0:T(8,128)}, f32[32,64]{1,0:T(8,128)S(1)}, u32[]{:S(2)}) copy-start(f32[32,64]{1,0:T(8,128)S(1)} %get-tuple-element.1572) | copy-start | bytes 24580
  11.6 125.6 %copy-start.11 = (f32[32,64]{1,0:T(8,128)}, f32[32,64]{1,0:T(8,128)S(1)}, u32[]{:S(2)}) copy-start(f32[32,64]{1,0:T(8,128)S(1)} %get-tuple-element.1573) | copy-start | bytes 24580
  12.5 239.9 %all-gather.7.cloned.1.call-start = ((), (), s32[]{:S(2)}) async-start(), calls=%async_computation.3 | async-start | bytes 2129920 | tf_op jit(solution)/shard_map/all_gather | solution.py:66
  13.3 752.5 %reduce-scatter.2.cloned.1.call-start = ((), (), s32[]{:S(2)}) async-start(), calls=%async_computation.2 | async-start | bytes 8519680 | tf_op jit(solution)/shard_map/reduce_scatter | solution.py:226
  16.3 121.0 %copy-start.20 = (f32[32]{0:T(128)}, f32[32]{0:T(128)S(1)}, u32[]{:S(2)}) copy-start(f32[32]{0:T(128)S(1)} %fusion.159) | copy-start | bytes 388
  283.1 3.9 copy-start.7
  283.1 3.9 copy-start.13
  283.1 11.5 %copy-start.1 = (bf16[2,16,4,4,128]{4,1,3,2,0:T(8,128)(2,1)}, bf16[2,16,4,4,128]{4,1,3,2,0:T(8,128)(2,1)S(1)}, u32[]{:S(2)}) copy-start(bf16[2,16,4,4,128]{4,1,3,2,0:T(8,128)(2,1)S(1)} %get-tuple-element.2072) | copy-start | bytes 393220 | tf_op jit(solution)/shard_map/while
  283.1 11.5 %copy-start.5 = (f32[2,4,4,16]{3,2,1,0:T(4,128)}, f32[2,4,4,16]{3,2,1,0:T(4,128)S(1)}, u32[]{:S(2)}) copy-start(f32[2,4,4,16]{3,2,1,0:T(4,128)S(1)} %get-tuple-element.2075) | copy-start | bytes 6148 | tf_op jit(solution)/shard_map/while
  283.1 11.5 %copy-start.18 = (s32[2,16]{1,0:T(2,128)}, s32[2,16]{1,0:T(2,128)S(1)}, u32[]{:S(2)}) copy-start(s32[2,16]{1,0:T(2,128)S(1)} %get-tuple-element.2071) | copy-start | bytes 388 | tf_op jit(solution)/shard_map/while
  284.4 2.5 copy-start.4
  307.0 1.6 copy-start.2
  307.1 1.5 copy-start.6
  307.1 1.5 copy-start.8
  307.1 1.5 copy-start.14
  308.6 3.9 copy-start.7
  308.6 3.9 copy-start.13
  308.6 7.4 copy-start.1
  308.7 7.4 copy-start.5
  308.7 7.4 copy-start.18
  310.0 2.5 copy-start.4
  319.5 1.5 copy-start.2
  319.5 1.5 copy-start.6
  321.1 3.9 copy-start.7
  321.1 3.9 copy-start.13
  321.1 7.4 copy-start.1
  321.1 7.4 copy-start.5
  321.1 7.4 copy-start.18
  322.5 2.5 copy-start.4
  332.0 1.5 copy-start.2
  333.5 3.9 copy-start.7
  333.6 3.9 copy-start.13
  333.6 7.4 copy-start.1
  333.6 7.4 copy-start.5
  333.6 7.4 copy-start.18
  334.9 2.5 copy-start.4
  344.4 1.7 copy-start.2
  344.5 1.7 copy-start.6
  344.5 1.6 copy-start.8
  344.5 1.6 copy-start.14
  344.5 1.6 copy-start.19
  346.8 25.7 %copy-start.10 = (f32[32,64]{1,0:T(8,128)S(1)}, f32[32,64]{1,0:T(8,128)}, u32[]{:S(2)}) copy-start(f32[32,64]{1,0:T(8,128)} %copy-done.9) | copy-start | bytes 24580
  346.8 25.7 %copy-start.12 = (f32[32,64]{1,0:T(8,128)S(1)}, f32[32,64]{1,0:T(8,128)}, u32[]{:S(2)}) copy-start(f32[32,64]{1,0:T(8,128)} %copy-done.11) | copy-start | bytes 24580
  (12 other events, 16.2 us)
Sparse Core Ops, SparseCore 0:
  12.6 120.6 all-gather.4
  136.9 115.4 all-gather.6
  346.3 419.4 reduce-scatter.1
where the time goes:
time: 779 us; the launch traced here: 775 us
  waiting for transfers between devices  438 us (56%)
  blocking collectives  150 us (19%)
  local copies, waits for them, and re-layouts  100 us (13%)
  loops' own time  42.3 us (5%)
  other arithmetic  20 us (3%)
  between operations  14.7 us (2%)
  matrix products  10.6 us (1%)
    reduce_scatter x1, waiting for transfers between devices, shards(): lax.psum_scatter(lax.fori_loop(0, lax.axis_size('ctx') * slots // tile_ro...  269 us
    psum x1, blocking collectives, shards(): router_total = lax.psum(router_part, ('dp', 'ctx'))  122 us
    all_gather x1, waiting for transfers between devices, shards(): lax.all_gather(key_rot, 'ctx', axis=0, tiled=True)  88.7 us
    all_gather x1, waiting for transfers between devices, shards(): lax.all_gather(values[0], 'ctx', axis=0, tiled=True)  79.1 us
    all_gather x1, blocking collectives, shards(): lax.all_gather(own_places, 'ctx', axis=0, tiled=True)  27.9 us
  transfers between devices with their start and end apart: 3, of which 3 were waited for; matrix products, arithmetic and copies ran while one was open for 6% of the time, Pallas kernels for 0%

commit v1 on v0

v1 whole, which is shorter than its diff:
```python
import math

import jax
import jax.numpy as jnp
import numpy as np
from jax import lax
from jax.experimental import pallas as pl
from jax.experimental.pallas import tpu as pltpu
from jax.sharding import PartitionSpec as P

HQ = 16
KVH = 4
HD = 128
ROPE_BASE = 500000.0
SCORE_SCALE = 1.0 / math.sqrt(HD)
MESH = pl.DeviceIdType.MESH

ROWS = 32
QUAD = 4
MATES = 16
SUPER = 8
SLOT = QUAD * ROWS
SPAN = 2 * SLOT
GROUP = HQ // KVH
QROWS = GROUP * SLOT
NEG = -1e30
F32 = jnp.float32
BF16 = jnp.bfloat16


def rope_rows():
    pairs = HD // 2
    frequency = [ROPE_BASE ** (-number / pairs) for number in range(pairs)]
    coarse = [256.0 * factor % (2.0 * math.pi) for factor in frequency]
    table = np.zeros((8, HD), np.float32)
    table[0] = np.asarray(frequency + frequency, np.float32)
    table[1] = np.asarray(coarse + coarse, np.float32)
    return table


def nt(left, right):
    return lax.dot_general(left, right, (((1,), (1,)), ((), ())), preferred_element_type=F32)


def tn(left, right):
    return lax.dot_general(left, right, (((0,), (0,)), ((), ())), preferred_element_type=F32)


def kernel(
    q_ref, k_ref, v_ref, g_ref, x_ref, w_ref, p_ref, rope_ref,
    dq_out, dk_out, dv_out, r_out,
    cos_s, sin_s, gate_s, kv4, qg4, kv, qg, q_s, g_s, s_s, d_s, dqt_s, pb, rb, dqs, dqr, cb, kr,
    ts, tr, rp, r1, r2s, r2, r3s, r3, r4,
    kv_ss, kv_rs, qg_ss, qg_rs, ga_ss, ga_rs, pb_ss, pb_rs, dq_ss, dq_rs, kr_ss, kr_rs,
    t_ss, t_rs, r1_ss, r1_rs, r2_ss, r2_rs, r3_ss, r3_rs, r4_ss, r4_rs,
):
    dp = lax.axis_index("dp")
    ctx = lax.axis_index("ctx")
    run = ctx // 8
    z = ctx % 8
    head = z // 2
    par = z % 2
    mate = run * 2 + par

    def quad_at(member):
        return (dp, run * 8 + 2 * member + par)

    def mate_at(index):
        return (dp, (index // 2) * 8 + 2 * head + index % 2)

    def dp_at(index):
        return (index, ctx)

    def remote(src, dst, send, recv, to):
        return pltpu.make_async_remote_copy(
            src_ref=src, dst_ref=dst, send_sem=send, recv_sem=recv, device_id=to, device_id_type=MESH
        )

    def other(step):
        return lax.rem(head + step, QUAD)

    def other_dp(step):
        return lax.rem(dp + step, 4)

    barrier = pltpu.get_barrier_semaphore()
    for step in range(1, QUAD):
        pl.semaphore_signal(barrier, inc=1, device_id=quad_at(other(step)), device_id_type=MESH)
        pl.semaphore_signal(barrier, inc=1, device_id=dp_at(other_dp(step)), device_id_type=MESH)

    def greet(step, carry):
        pl.semaphore_signal(
            barrier, inc=1, device_id=mate_at(lax.rem(mate + step, MATES)), device_id_type=MESH
        )
        return carry

    lax.fori_loop(1, MATES, greet, 0)

    eye = lax.broadcasted_iota(jnp.int32, (ROWS, ROWS), 0) == lax.broadcasted_iota(
        jnp.int32, (ROWS, ROWS), 1
    )
    places = jnp.broadcast_to(p_ref[...], (ROWS, ROWS))
    upper = jnp.sum(jnp.where(eye, (places >> 8).astype(F32), 0.0), axis=1, keepdims=True)
    lower = jnp.sum(jnp.where(eye, (places & 255).astype(F32), 0.0), axis=1, keepdims=True)
    angles = upper * rope_ref[1:2, :] + lower * rope_ref[0:1, :]
    lane = lax.broadcasted_iota(jnp.int32, (ROWS, HD), 1)
    cos = jnp.cos(angles)
    sin = jnp.sin(angles)
    sin = jnp.where(lane < HD // 2, -sin, sin)
    cos_s[...] = cos
    sin_s[...] = sin

    def turn(rows):
        return rows * cos + pltpu.roll(rows, HD // 2, 1) * sin

    for number in range(KVH):
        cols = slice(number * HD, (number + 1) * HD)
        kv4[number, :, :HD] = turn(k_ref[:, cols].astype(F32)).astype(BF16)
        kv4[number, :, HD:] = v_ref[:, cols]

    pl.semaphore_wait(barrier, 2 * (QUAD - 1) + MATES - 1)

    def kv_copy(step):
        to = other(step)
        return remote(
            kv4.at[to], kv.at[mate, pl.ds(head * ROWS, ROWS)], kv_ss.at[step], kv_rs.at[step], quad_at(to)
        )

    for step in range(1, QUAD):
        kv_copy(step).start()
    kv[mate, pl.ds(pl.multiple_of(head * ROWS, ROWS), ROWS)] = kv4[head]

    logits = jnp.sum(x_ref[...].astype(F32) * w_ref[...], axis=1, keepdims=True)
    gate = jax.nn.sigmoid(logits)
    gate_s[...] = jnp.broadcast_to(gate, (ROWS, HD))
    for number in range(HQ):
        cols = slice(number * HD, (number + 1) * HD)
        part, into = number // GROUP, slice((number % GROUP) * HD, (number % GROUP + 1) * HD)
        qg4[part, 0, :, into] = turn(q_ref[:, cols].astype(F32)).astype(BF16)
        qg4[part, 1, :, into] = (gate * g_ref[:, cols].astype(F32)).astype(BF16)

    def qg_copy(step):
        to = other(step)
        return remote(qg4.at[to], qg.at[head], qg_ss.at[step], qg_rs.at[step], quad_at(to))

    for step in range(1, QUAD):
        qg_copy(step).start()
    qg[head] = qg4[head]

    for step in range(1, QUAD):
        kv_copy(step).wait_recv()

    def ga_send(index):
        return remote(kv.at[mate], kv.at[mate], ga_ss.at[index], ga_rs.at[mate], mate_at(index))

    def ga_recv(index):
        return remote(kv.at[mate], kv.at[index], ga_ss.at[index], ga_rs.at[index], mate_at(index))

    def ga_start(index, carry):
        @pl.when(index != mate)
        def _():
            ga_send(index).start()

        return carry

    lax.fori_loop(run * 2, MATES, ga_start, 0)

    for step in range(1, QUAD):
        qg_copy(step).wait_recv()
    for number in range(GROUP):
        cols = slice(number * HD, (number + 1) * HD)
        q_s[number * SLOT : (number + 1) * SLOT, :] = qg[:, 0, :, cols].reshape(SLOT, HD)
        g_s[number * SLOT : (number + 1) * SLOT, :] = qg[:, 1, :, cols].reshape(SLOT, HD)

    key_at = lax.broadcasted_iota(jnp.int32, (SPAN, QROWS), 0)
    key_at = (key_at >> 7) * ROWS + ((key_at & 96) << 1) + (key_at & 31)
    row_at = lax.broadcasted_iota(jnp.int32, (SPAN, QROWS), 1)
    row_at = par * ROWS + ((row_at & 96) << 1) + (row_at & 31)
    ahead = key_at - row_at

    def score_step(number, top):
        for side in range(2):
            index = 2 * number + side

            @pl.when(index != mate)
            def _():
                ga_recv(index).wait_recv()

        both = jnp.concatenate([kv[2 * number], kv[2 * number + 1]], axis=0)
        scores = nt(both[:, :HD], q_s[...]) * (SCORE_SCALE * math.log2(math.e))
        scores = jnp.where(ahead <= (run - number) * SPAN, scores, NEG)
        s_s[number] = scores
        d_s[number] = nt(both[:, HD:], g_s[...]) * SCORE_SCALE
        return jnp.maximum(top, jnp.max(scores, axis=0, keepdims=True))

    top = lax.fori_loop(0, run + 1, score_step, jnp.full((1, QROWS), NEG, F32))

    def mass_step(number, carry):
        mass, pull = carry
        raised = jnp.exp2(s_s[number] - top)
        s_s[number] = raised
        return (
            mass + jnp.sum(raised, axis=0, keepdims=True),
            pull + jnp.sum(raised * d_s[number], axis=0, keepdims=True),
        )

    zero_row = jnp.zeros((1, QROWS), F32)
    mass, pull = lax.fori_loop(0, run + 1, mass_step, (zero_row, zero_row))
    inverse = 1.0 / mass
    delta = pull * inverse

    term = delta[:, :SLOT]
    for number in range(1, GROUP):
        term = term + delta[:, number * SLOT : (number + 1) * SLOT]
    ts[...] = jnp.broadcast_to(term * math.sqrt(HD), (8, SLOT))

    def t_copy(step):
        return remote(ts, tr.at[head], t_ss.at[step], t_rs.at[step], quad_at(other(step)))

    for step in range(1, QUAD):
        t_copy(step).start()
    tr[head] = ts[...]

    def pb_send(index):
        return remote(pb.at[index], rb.at[mate], pb_ss.at[index], pb_rs.at[mate], mate_at(index))

    def pb_recv(index):
        return remote(pb.at[index], rb.at[index], pb_ss.at[index], pb_rs.at[index], mate_at(index))

    dqt_s[...] = jnp.zeros_like(dqt_s)

    def grad_step(number, carry):
        weights = s_s[number] * inverse
        probs = weights.astype(BF16)
        slope = (weights * (d_s[number] - delta)).astype(BF16)
        keys = jnp.concatenate([kv[2 * number, :, :HD], kv[2 * number + 1, :, :HD]], axis=0)
        dk = jnp.dot(slope, q_s[...], preferred_element_type=F32)
        dv = jnp.dot(probs, g_s[...], preferred_element_type=F32)
        grads = jnp.concatenate([dk, dv], axis=1).astype(BF16)
        for side in range(2):
            index = 2 * number + side
            pb[index] = grads[side * SLOT : (side + 1) * SLOT]

            @pl.when(index != mate)
            def _():
                pb_send(index).start()

        dqt_s[...] += tn(keys, slope)
        return carry

    lax.fori_loop(0, run + 1, grad_step, 0)
    rb[mate] = pb[mate]

    turned = dqt_s[...].T.astype(BF16)
    for number in range(GROUP):
        cols = slice(number * HD, (number + 1) * HD)
        dqs[:, :, cols] = turned[number * SLOT : (number + 1) * SLOT].reshape(QUAD, ROWS, HD)

    def dq_copy(step):
        to = other(step)
        return remote(dqs.at[to], dqr.at[head], dq_ss.at[step], dq_rs.at[step], quad_at(to))

    for step in range(1, QUAD):
        dq_copy(step).start()
    dqr[head] = dqs[head]

    for step in range(1, QUAD):
        t_copy(step).wait_recv()
    term = tr[0, 0:1] + tr[1, 0:1] + tr[2, 0:1] + tr[3, 0:1]
    spot = lax.broadcasted_iota(jnp.int32, (ROWS, SLOT), 0) + head * ROWS
    pick = lax.broadcasted_iota(jnp.int32, (ROWS, SLOT), 1) == spot
    term = jnp.sum(jnp.where(pick, jnp.broadcast_to(term, (ROWS, SLOT)), 0.0), axis=1, keepdims=True)
    logit_grad = (1.0 - gate_s[:, 0:1]) * term
    part = jnp.sum(logit_grad * x_ref[...].astype(F32), axis=0, keepdims=True)
    for number in range(32):
        rp[number : number + 1, :] = part[:, number * 128 : (number + 1) * 128]

    def r1_copy(step):
        to = other(step)
        return remote(
            rp.at[pl.ds(pl.multiple_of(to * 8, 8), 8)], r1.at[head], r1_ss.at[step], r1_rs.at[step], quad_at(to)
        )

    for step in range(1, QUAD):
        r1_copy(step).start()
    r1[head] = rp[pl.ds(pl.multiple_of(head * 8, 8), 8)]
    for step in range(1, QUAD):
        r1_copy(step).wait_recv()
    r2s[...] = r1[0] + r1[1] + r1[2] + r1[3]

    def r2_send(index):
        return remote(r2s, r2.at[mate], r2_ss.at[index], r2_rs.at[mate], mate_at(index))

    def r2_recv(index):
        return remote(r2s, r2.at[index], r2_ss.at[index], r2_rs.at[index], mate_at(index))

    def r2_start(index, carry):
        @pl.when(index != mate)
        def _():
            r2_send(index).start()

        return carry

    lax.fori_loop(0, MATES, r2_start, 0)
    r2[mate] = r2s[...]

    def gather_sum(index, total):
        @pl.when(index != mate)
        def _():
            pb_recv(index).wait_recv()

        return total + rb[index].astype(F32)

    total = lax.fori_loop(run * 2, MATES, gather_sum, jnp.zeros((SLOT, 2 * HD), F32))
    cb[...] = total.astype(BF16)

    def kr_copy(step):
        to = other(step)
        return remote(
            cb.at[pl.ds(pl.multiple_of(to * ROWS, ROWS), ROWS)], kr.at[head], kr_ss.at[step], kr_rs.at[step],
            quad_at(to),
        )

    for step in range(1, QUAD):
        kr_copy(step).start()
    kr[head] = cb[pl.ds(pl.multiple_of(head * ROWS, ROWS), ROWS)]

    def r2_sum(index, total):
        @pl.when(index != mate)
        def _():
            r2_recv(index).wait_recv()

        return total + r2[index]

    r3s[...] = lax.fori_loop(0, MATES, r2_sum, jnp.zeros((8, 128), F32))

    def r3_copy(step):
        return remote(r3s, r3.at[dp], r3_ss.at[step], r3_rs.at[step], dp_at(other_dp(step)))

    for step in range(1, 4):
        r3_copy(step).start()
    r3[dp] = r3s[...]

    back_cos = cos_s[...]
    back_sin = sin_s[...]

    def turn_back(rows):
        return rows * back_cos - pltpu.roll(rows, HD // 2, 1) * back_sin

    for step in range(1, QUAD):
        dq_copy(step).wait_recv()
    for number in range(HQ):
        cols = slice((number % GROUP) * HD, (number % GROUP + 1) * HD)
        rows = dqr[number // GROUP, :, cols].astype(F32)
        dq_out[:, number * HD : (number + 1) * HD] = turn_back(rows).astype(BF16)

    for step in range(1, 4):
        r3_copy(step).wait_recv()
    own = pl.ds(pl.multiple_of(head * 8, 8), 8)
    r4[own] = (r3[0] + r3[1] + r3[2] + r3[3]) * (1.0 / math.sqrt(4 * 2048))

    def r4_copy(step):
        return remote(r4.at[own], r4.at[own], r4_ss.at[step], r4_rs.at[step], quad_at(other(step)))

    for step in range(1, QUAD):
        r4_copy(step).start()

    for step in range(1, QUAD):
        kr_copy(step).wait_recv()
    for number in range(KVH):
        cols = slice(number * HD, (number + 1) * HD)
        dk_out[:, cols] = turn_back(kr[number, :, :HD].astype(F32)).astype(BF16)
        dv_out[:, cols] = kr[number, :, HD:]

    for step in range(1, QUAD):
        r4_copy(step).wait_recv()
    r_out[...] = r4[...]

    for step in range(1, QUAD):
        for copy in (kv_copy, qg_copy, t_copy, dq_copy, r1_copy, kr_copy, r3_copy, r4_copy):
            copy(step).wait_send()

    def drain_late(index, carry):
        @pl.when(index != mate)
        def _():
            ga_send(index).wait_send()

        return carry

    lax.fori_loop(run * 2, MATES, drain_late, 0)

    def drain_early(index, carry):
        @pl.when(index != mate)
        def _():
            pb_send(index).wait_send()

        return carry

    lax.fori_loop(0, run * 2 + 2, drain_early, 0)

    def drain_all(index, carry):
        @pl.when(index != mate)
        def _():
            r2_send(index).wait_send()

        return carry

    lax.fori_loop(0, MATES, drain_all, 0)


def shards(queries, keys, values, out_grad, routed_inputs, router_weight, positions):
    vmem = pl.BlockSpec(memory_space=pltpu.VMEM)
    dma = pltpu.SemaphoreType.DMA
    scratch = [
        pltpu.VMEM((ROWS, HD), F32),
        pltpu.VMEM((ROWS, HD), F32),
        pltpu.VMEM((ROWS, HD), F32),
        pltpu.VMEM((KVH, ROWS, 2 * HD), BF16),
        pltpu.VMEM((QUAD, 2, ROWS, GROUP * HD), BF16),
        pltpu.VMEM((MATES, SLOT, 2 * HD), BF16),
        pltpu.VMEM((QUAD, 2, ROWS, GROUP * HD), BF16),
        pltpu.VMEM((QROWS, HD), BF16),
        pltpu.VMEM((QROWS, HD), BF16),
        pltpu.VMEM((SUPER, SPAN, QROWS), F32),
        pltpu.VMEM((SUPER, SPAN, QROWS), F32),
        pltpu.VMEM((HD, QROWS), F32),
        pltpu.VMEM((MATES, SLOT, 2 * HD), BF16),
        pltpu.VMEM((MATES, SLOT, 2 * HD), BF16),
        pltpu.VMEM((QUAD, ROWS, GROUP * HD), BF16),
        pltpu.VMEM((QUAD, ROWS, GROUP * HD), BF16),
        pltpu.VMEM((SLOT, 2 * HD), BF16),
        pltpu.VMEM((QUAD, ROWS, 2 * HD), BF16),
        pltpu.VMEM((8, 128), F32),
        pltpu.VMEM((QUAD, 8, 128), F32),
        pltpu.VMEM((32, 128), F32),
        pltpu.VMEM((QUAD, 8, 128), F32),
        pltpu.VMEM((8, 128), F32),
        pltpu.VMEM((MATES, 8, 128), F32),
        pltpu.VMEM((8, 128), F32),
        pltpu.VMEM((4, 8, 128), F32),
        pltpu.VMEM((32, 128), F32),
        dma((QUAD,)), dma((QUAD,)), dma((QUAD,)), dma((QUAD,)),
        dma((MATES,)), dma((MATES,)), dma((MATES,)), dma((MATES,)),
        dma((QUAD,)), dma((QUAD,)), dma((QUAD,)), dma((QUAD,)),
        dma((QUAD,)), dma((QUAD,)), dma((QUAD,)), dma((QUAD,)),
        dma((MATES,)), dma((MATES,)), dma((QUAD,)), dma((QUAD,)),
        dma((QUAD,)), dma((QUAD,)),
    ]
    query_grad, key_grad, value_grad, router = pl.pallas_call(
        kernel,
        out_shape=(
            jax.ShapeDtypeStruct((ROWS, HQ * HD), BF16),
            jax.ShapeDtypeStruct((ROWS, KVH * HD), BF16),
            jax.ShapeDtypeStruct((ROWS, KVH * HD), BF16),
            jax.ShapeDtypeStruct((32, 128), F32),
        ),
        in_specs=[vmem] * 8,
        out_specs=(vmem,) * 4,
        scratch_shapes=scratch,
        compiler_params=pltpu.CompilerParams(
            collective_id=0, has_side_effects=True, vmem_limit_bytes=40 * 1024 * 1024
        ),
    )(
        queries[0],
        keys[0],
        values[0],
        out_grad[0],
        routed_inputs[0],
        router_weight.reshape(1, -1),
        positions,
        jnp.asarray(rope_rows()),
    )
    return (query_grad[None], key_grad[None], value_grad[None], router.reshape(-1))


def solution(mesh):
    row = P("dp", "ctx", None)
    in_specs = (row, row, row, row, row, P(), P("dp", "ctx"))
    out_specs = (row, row, row, P())
    return jax.shard_map(shards, mesh=mesh, in_specs=in_specs, out_specs=out_specs, check_vma=False)
```

time: 779 us -> 77.1 us (0.10)
  the two profiles are of different devices: /device:TPU:2 before, /device:TPU:1 now
where the time goes in v1:
time: 77.1 us; the launch traced here: 76.7 us
  Pallas kernels  67.9 us (88%)
  local copies, waits for them, and re-layouts  8.16 us (11%)
    pallas_call x1, Pallas kernels, shards(): pl.pallas_call(kernel, out_shape=(jax.ShapeDtypeStruct((ROWS, HQ * HD), B...  67.9 us
    unnamed x20, local copies, waits for them, and re-layouts  8.16 us

profile of v1, /device:TPU:1, one launch (start us, length us, event | category | flops | bytes accessed | tf_op | source)
XLA Modules:
  0.0 76.7 jit_solution(10365825525224323646)
XLA Ops:
  0.6 0.0 copy-start.6
  0.6 0.0 copy-start.7
  0.7 0.7 copy-done.6
  1.3 0.0 copy-done.7
  1.3 0.0 copy-start
  1.3 0.9 %copy-done = bf16[1,32,4096]{2,1,0:T(8,128)(2,1)S(1)} copy-done((bf16[1,32,4096]{2,1,0:T(8,128)(2,1)S(1)}, bf16[1,32,4096]{2,1,0:T(8,128)(2,1)}, u32[]{:S(2)}) %copy-start) | copy-done | bytes 262168
  2.3 0.0 copy-start.1
  2.3 0.9 %copy-done.1 = bf16[1,32,2048]{2,1,0:T(8,128)(2,1)S(1)} copy-done((bf16[1,32,2048]{2,1,0:T(8,128)(2,1)S(1)}, bf16[1,32,2048]{2,1,0:T(8,128)(2,1)}, u32[]{:S(2)}) %copy-start.1) | copy-done | bytes 131096
  3.2 0.0 copy-start.2
  3.2 0.9 %copy-done.2 = bf16[1,32,2048]{2,1,0:T(8,128)(2,1)S(1)} copy-done((bf16[1,32,2048]{2,1,0:T(8,128)(2,1)S(1)}, bf16[1,32,2048]{2,1,0:T(8,128)(2,1)}, u32[]{:S(2)}) %copy-start.2) | copy-done | bytes 131096
  4.1 0.0 copy-start.3
  4.1 0.8 copy-done.3
  4.8 0.0 copy-start.4
  4.8 0.8 copy-done.4
  5.6 0.0 copy-start.5
  5.6 0.7 copy-done.5
  6.3 67.9 %shard_map.111 = (bf16[32,2048]{1,0:T(8,128)(2,1)S(1)}, bf16[32,512]{1,0:T(8,128)(2,1)S(1)}, bf16[32,512]{1,0:T(8,128)(2,1)S(1)}, f32[32,128]{1,0:T(8,128)S(1)}) custom-call(bf16[32,2048]{1,0:T(8,128)(2,1)S(1)} %bitcast.12, bf16[32,512]{1,0:T(8,128)(2,1)S(1)} %bitcast.14, bf16[32,512]{1,0:T(8,128)(2,1)S(1)} %bitcast.15, bf16[32,2048]{1,0:T(8,128)(2,1)S(1)} %bitcast.13, ...), custom_call_target="tpu_custom_call" | custom-call | tf_op jit(solution)/shard_map/pallas_call | solution.py:448
  74.2 0.7 copy.16
  74.9 0.6 copy.17
  75.5 0.6 copy.18
  76.1 0.6 copy.19
Async XLA Ops:
  0.6 0.7 copy-start.6
  0.6 0.7 copy-start.7
  1.3 1.0 %copy-start = (bf16[1,32,4096]{2,1,0:T(8,128)(2,1)S(1)}, bf16[1,32,4096]{2,1,0:T(8,128)(2,1)}, u32[]{:S(2)}) copy-start(bf16[1,32,4096]{2,1,0:T(8,128)(2,1)} %param.12) | copy-start | bytes 786436
  2.3 0.9 %copy-start.1 = (bf16[1,32,2048]{2,1,0:T(8,128)(2,1)S(1)}, bf16[1,32,2048]{2,1,0:T(8,128)(2,1)}, u32[]{:S(2)}) copy-start(bf16[1,32,2048]{2,1,0:T(8,128)(2,1)} %param.8) | copy-start | bytes 393220
  3.2 0.9 %copy-start.2 = (bf16[1,32,2048]{2,1,0:T(8,128)(2,1)S(1)}, bf16[1,32,2048]{2,1,0:T(8,128)(2,1)}, u32[]{:S(2)}) copy-start(bf16[1,32,2048]{2,1,0:T(8,128)(2,1)} %param.11) | copy-start | bytes 393220
  4.1 0.8 copy-start.3
  4.8 0.8 copy-start.4
  5.6 0.7 copy-start.5

commit v2 on v1

--- a/solution.py
+++ b/solution.py
@@ -47,10 +47,10 @@
 
 
 def kernel(
-    q_ref, k_ref, v_ref, g_ref, x_ref, w_ref, p_ref, rope_ref,
-    dq_out, dk_out, dv_out, r_out,
-    cos_s, sin_s, gate_s, kv4, qg4, kv, qg, q_s, g_s, s_s, d_s, dqt_s, pb, rb, dqs, dqr, cb, kr,
-    ts, tr, rp, r1, r2s, r2, r3s, r3, r4,
+    q_hbm, k_hbm, v_hbm, g_hbm, x_hbm, w_hbm, p_hbm, rope_hbm,
+    dqr, kr, cos_s, sin_s, r4,
+    q_ref, k_ref, v_ref, g_ref, x_ref, w_ref, p_ref, rope_ref, in_sem, gate_s, kv4, qg4, kv, qg, q_s, g_s, s_s, d_s, dqt_s, pb, rb, dqs, cb,
+    ts, tr, rp, r1, r2s, r2, r3s, r3,
     kv_ss, kv_rs, qg_ss, qg_rs, ga_ss, ga_rs, pb_ss, pb_rs, dq_ss, dq_rs, kr_ss, kr_rs,
     t_ss, t_rs, r1_ss, r1_rs, r2_ss, r2_rs, r3_ss, r3_rs, r4_ss, r4_rs,
 ):
@@ -94,6 +94,18 @@
         return carry
 
     lax.fori_loop(1, MATES, greet, 0)
+
+    pairs = (
+        (p_hbm, p_ref), (rope_hbm, rope_ref), (k_hbm, k_ref), (v_hbm, v_ref),
+        (x_hbm, x_ref), (w_hbm, w_ref), (q_hbm, q_ref), (g_hbm, g_ref),
+    )
+    fetches = [
+        pltpu.make_async_copy(src, dst, in_sem.at[number]) for number, (src, dst) in enumerate(pairs)
+    ]
+    for fetch in fetches:
+        fetch.start()
+    fetches[0].wait()
+    fetches[1].wait()
 
     eye = lax.broadcasted_iota(jnp.int32, (ROWS, ROWS), 0) == lax.broadcasted_iota(
         jnp.int32, (ROWS, ROWS), 1
@@ -112,6 +124,8 @@
     def turn(rows):
         return rows * cos + pltpu.roll(rows, HD // 2, 1) * sin
 
+    fetches[2].wait()
+    fetches[3].wait()
     for number in range(KVH):
         cols = slice(number * HD, (number + 1) * HD)
         kv4[number, :, :HD] = turn(k_ref[:, cols].astype(F32)).astype(BF16)
@@ -129,6 +143,8 @@
         kv_copy(step).start()
     kv[mate, pl.ds(pl.multiple_of(head * ROWS, ROWS), ROWS)] = kv4[head]
 
+    for fetch in fetches[4:]:
+        fetch.wait()
     logits = jnp.sum(x_ref[...].astype(F32) * w_ref[...], axis=1, keepdims=True)
     gate = jax.nn.sigmoid(logits)
     gate_s[...] = jnp.broadcast_to(gate, (ROWS, HD))
@@ -177,7 +193,8 @@
     row_at = par * ROWS + ((row_at & 96) << 1) + (row_at & 31)
     ahead = key_at - row_at
 
-    def score_step(number, top):
+    def score_step(back, top):
+        number = run - back
         for side in range(2):
             index = 2 * number + side
 
@@ -247,8 +264,53 @@
         dqt_s[...] += tn(keys, slope)
         return carry
 
-    lax.fori_loop(0, run + 1, grad_step, 0)
-    rb[mate] = pb[mate]
+    half = (run + 1) // 2
+    lax.fori_loop(0, half, grad_step, 0)
+
+    for step in range(1, QUAD):
+        t_copy(step).wait_recv()
+    term = tr[0] + tr[1] + tr[2] + tr[3]
+    spot = lax.broadcasted_iota(jnp.int32, (ROWS, SLOT), 0) + head * ROWS
+    pick = lax.broadcasted_iota(jnp.int32, (ROWS, SLOT), 1) == spot
+    term = jnp.concatenate([term] * (ROWS // 8), axis=0)
+    term = jnp.sum(jnp.where(pick, term, 0.0), axis=1, keepdims=True)
+    logit_grad = (1.0 - gate_s[:, 0:1]) * term
+    part = jnp.sum(logit_grad * x_ref[...].astype(F32), axis=0, keepdims=True)
+    for number in range(32):
+        rp[number : number + 1, :] = part[:, number * 128 : (number + 1) * 128]
+
+    own = pl.ds(pl.multiple_of(head * 8, 8), 8)
+
+    def r1_copy(step):
+        to = other(step)
+        rows = pl.ds(pl.multiple_of(to * 8, 8), 8)
+        return remote(rp.at[rows], r1.at[head], r1_ss.at[step], r1_rs.at[step], quad_at(to))
+
+    for step in range(1, QUAD):
+        r1_copy(step).start()
+    r1[head] = rp[own]
+
+    lax.fori_loop(half, run + 1, grad_step, 0)
+
+    for step in range(1, QUAD):
+        r1_copy(step).wait_recv()
+    r2s[...] = r1[0] + r1[1] + r1[2] + r1[3]
+
+    def r2_send(index):
+        return remote(r2s, r2.at[mate], r2_ss.at[index], r2_rs.at[mate], mate_at(index))
+
+    def r2_recv(index):
+        return remote(r2s, r2.at[index], r2_ss.at[index], r2_rs.at[index], mate_at(index))
+
+    def r2_start(index, carry):
+        @pl.when(index != mate)
+        def _():
+            r2_send(index).start()
+
+        return carry
+
+    lax.fori_loop(0, MATES, r2_start, 0)
+    r2[mate] = r2s[...]
 
     turned = dqt_s[...].T.astype(BF16)
     for number in range(GROUP):
@@ -263,45 +325,7 @@
         dq_copy(step).start()
     dqr[head] = dqs[head]
 
-    for step in range(1, QUAD):
-        t_copy(step).wait_recv()
-    term = tr[0, 0:1] + tr[1, 0:1] + tr[2, 0:1] + tr[3, 0:1]
-    spot = lax.broadcasted_iota(jnp.int32, (ROWS, SLOT), 0) + head * ROWS
-    pick = lax.broadcasted_iota(jnp.int32, (ROWS, SLOT), 1) == spot
-    term = jnp.sum(jnp.where(pick, jnp.broadcast_to(term, (ROWS, SLOT)), 0.0), axis=1, keepdims=True)
-    logit_grad = (1.0 - gate_s[:, 0:1]) * term
-    part = jnp.sum(logit_grad * x_ref[...].astype(F32), axis=0, keepdims=True)
-    for number in range(32):
-        rp[number : number + 1, :] = part[:, number * 128 : (number + 1) * 128]
-
-    def r1_copy(step):
-        to = other(step)
-        return remote(
-            rp.at[pl.ds(pl.multiple_of(to * 8, 8), 8)], r1.at[head], r1_ss.at[step], r1_rs.at[step], quad_at(to)
-        )
-
-    for step in range(1, QUAD):
-        r1_copy(step).start()
-    r1[head] = rp[pl.ds(pl.multiple_of(head * 8, 8), 8)]
-    for step in range(1, QUAD):
-        r1_copy(step).wait_recv()
-    r2s[...] = r1[0] + r1[1] + r1[2] + r1[3]
-
-    def r2_send(index):
-        return remote(r2s, r2.at[mate], r2_ss.at[index], r2_rs.at[mate], mate_at(index))
-
-    def r2_recv(index):
-        return remote(r2s, r2.at[index], r2_ss.at[index], r2_rs.at[index], mate_at(index))
-
-    def r2_start(index, carry):
-        @pl.when(index != mate)
-        def _():
-            r2_send(index).start()
-
-        return carry
-
-    lax.fori_loop(0, MATES, r2_start, 0)
-    r2[mate] = r2s[...]
+    rb[mate] = pb[mate]
 
     def gather_sum(index, total):
         @pl.when(index != mate)
@@ -310,19 +334,8 @@
 
         return total + rb[index].astype(F32)
 
-    total = lax.fori_loop(run * 2, MATES, gather_sum, jnp.zeros((SLOT, 2 * HD), F32))
-    cb[...] = total.astype(BF16)
-
-    def kr_copy(step):
-        to = other(step)
-        return remote(
-            cb.at[pl.ds(pl.multiple_of(to * ROWS, ROWS), ROWS)], kr.at[head], kr_ss.at[step], kr_rs.at[step],
-            quad_at(to),
-        )
-
-    for step in range(1, QUAD):
-        kr_copy(step).start()
-    kr[head] = cb[pl.ds(pl.multiple_of(head * ROWS, ROWS), ROWS)]
+    middle = run + MATES // 2
+    total = lax.fori_loop(run * 2, middle, gather_sum, jnp.zeros((SLOT, 2 * HD), F32))
 
     def r2_sum(index, total):
         @pl.when(index != mate)
@@ -340,79 +353,97 @@
         r3_copy(step).start()
     r3[dp] = r3s[...]
 
-    back_cos = cos_s[...]
-    back_sin = sin_s[...]
+    total = lax.fori_loop(middle, MATES, gather_sum, total)
+    cb[...] = total.astype(BF16)
+
+    def kr_copy(step):
+        to = other(step)
+        rows = pl.ds(pl.multiple_of(to * ROWS, ROWS), ROWS)
+        return remote(cb.at[rows], kr.at[head], kr_ss.at[step], kr_rs.at[step], quad_at(to))
+
+    for step in range(1, QUAD):
+        kr_copy(step).start()
+    kr[head] = cb[pl.ds(pl.multiple_of(head * ROWS, ROWS), ROWS)]
+
+    for step in range(1, 4):
+        r3_copy(step).wait_recv()
+    r4[own] = (r3[0] + r3[1] + r3[2] + r3[3]) * (1.0 / math.sqrt(4 * 2048))
+
+    def r4_copy(step):
+        return remote(r4.at[own], r4.at[own], r4_ss.at[step], r4_rs.at[step], quad_at(other(step)))
+
+    for step in range(1, QUAD):
+        r4_copy(step).start()
+
+    for step in range(1, QUAD):
+        for copy in (kv_copy, qg_copy, t_copy, dq_copy, r1_copy, r3_copy):
+            copy(step).wait_send()
+
+    def drain_late(index, carry):
+        @pl.when(index != mate)
+        def _():
+            ga_send(index).wait_send()
+
+        return carry
+
+    lax.fori_loop(run * 2, MATES, drain_late, 0)
+
+    def drain_early(index, carry):
+        @pl.when(index != mate)
+        def _():
+            pb_send(index).wait_send()
+
+        return carry
+
+    lax.fori_loop(0, run * 2 + 2, drain_early, 0)
+
+    def drain_all(index, carry):
+        @pl.when(index != mate)
+        def _():
+            r2_send(index).wait_send()
+
+        return carry
+
+    lax.fori_loop(0, MATES, drain_all, 0)
+    for step in range(1, QUAD):
+        for copy in (dq_copy, kr_copy, r4_copy):
+            copy(step).wait_recv()
+        for copy in (kr_copy, r4_copy):
+            copy(step).wait_send()
+
+
+def finish(dqr, kr, cos_s, sin_s, r4, dq_out, dk_out, dv_out, r_out):
+    cos = cos_s[...]
+    sin = sin_s[...]
 
     def turn_back(rows):
-        return rows * back_cos - pltpu.roll(rows, HD // 2, 1) * back_sin
-
-    for step in range(1, QUAD):
-        dq_copy(step).wait_recv()
+        return rows * cos - pltpu.roll(rows, HD // 2, 1) * sin
+
     for number in range(HQ):
         cols = slice((number % GROUP) * HD, (number % GROUP + 1) * HD)
         rows = dqr[number // GROUP, :, cols].astype(F32)
         dq_out[:, number * HD : (number + 1) * HD] = turn_back(rows).astype(BF16)
-
-    for step in range(1, 4):
-        r3_copy(step).wait_recv()
-    own = pl.ds(pl.multiple_of(head * 8, 8), 8)
-    r4[own] = (r3[0] + r3[1] + r3[2] + r3[3]) * (1.0 / math.sqrt(4 * 2048))
-
-    def r4_copy(step):
-        return remote(r4.at[own], r4.at[own], r4_ss.at[step], r4_rs.at[step], quad_at(other(step)))
-
-    for step in range(1, QUAD):
-        r4_copy(step).start()
-
-    for step in range(1, QUAD):
-        kr_copy(step).wait_recv()
     for number in range(KVH):
         cols = slice(number * HD, (number + 1) * HD)
         dk_out[:, cols] = turn_back(kr[number, :, :HD].astype(F32)).astype(BF16)
         dv_out[:, cols] = kr[number, :, HD:]
-
-    for step in range(1, QUAD):
-        r4_copy(step).wait_recv()
     r_out[...] = r4[...]
-
-    for step in range(1, QUAD):
-        for copy in (kv_copy, qg_copy, t_copy, dq_copy, r1_copy, kr_copy, r3_copy, r4_copy):
-            copy(step).wait_send()
-
-    def drain_late(index, carry):
-        @pl.when(index != mate)
-        def _():
-            ga_send(index).wait_send()
-
-        return carry
-
-    lax.fori_loop(run * 2, MATES, drain_late, 0)
-
-    def drain_early(index, carry):
-        @pl.when(index != mate)
-        def _():
-            pb_send(index).wait_send()
-
-        return carry
-
-    lax.fori_loop(0, run * 2 + 2, drain_early, 0)
-
-    def drain_all(index, carry):
-        @pl.when(index != mate)
-        def _():
-            r2_send(index).wait_send()
-
-        return carry
-
-    lax.fori_loop(0, MATES, drain_all, 0)
 
 
 def shards(queries, keys, values, out_grad, routed_inputs, router_weight, positions):
     vmem = pl.BlockSpec(memory_space=pltpu.VMEM)
+    hbm = pl.BlockSpec(memory_space=pltpu.HBM)
     dma = pltpu.SemaphoreType.DMA
     scratch = [
-        pltpu.VMEM((ROWS, HD), F32),
-        pltpu.VMEM((ROWS, HD), F32),
+        pltpu.VMEM((ROWS, HQ * HD), BF16),
+        pltpu.VMEM((ROWS, KVH * HD), BF16),
+        pltpu.VMEM((ROWS, KVH * HD), BF16),
+        pltpu.VMEM((ROWS, HQ * HD), BF16),
+        pltpu.VMEM((ROWS, 4096), BF16),
+        pltpu.VMEM((1, 4096), F32),
+        pltpu.VMEM((1, ROWS), jnp.int32),
+        pltpu.VMEM((8, HD), F32),
+        dma((8,)),
         pltpu.VMEM((ROWS, HD), F32),
         pltpu.VMEM((KVH, ROWS, 2 * HD), BF16),
         pltpu.VMEM((QUAD, 2, ROWS, GROUP * HD), BF16),
@@ -426,9 +457,7 @@
         pltpu.VMEM((MATES, SLOT, 2 * HD), BF16),
         pltpu.VMEM((MATES, SLOT, 2 * HD), BF16),
         pltpu.VMEM((QUAD, ROWS, GROUP * HD), BF16),
-        pltpu.VMEM((QUAD, ROWS, GROUP * HD), BF16),
         pltpu.VMEM((SLOT, 2 * HD), BF16),
-        pltpu.VMEM((QUAD, ROWS, 2 * HD), BF16),
         pltpu.VMEM((8, 128), F32),
         pltpu.VMEM((QUAD, 8, 128), F32),
         pltpu.VMEM((32, 128), F32),
@@ -437,7 +466,6 @@
         pltpu.VMEM((MATES, 8, 128), F32),
         pltpu.VMEM((8, 128), F32),
         pltpu.VMEM((4, 8, 128), F32),
-        pltpu.VMEM((32, 128), F32),
         dma((QUAD,)), dma((QUAD,)), dma((QUAD,)), dma((QUAD,)),
         dma((MATES,)), dma((MATES,)), dma((MATES,)), dma((MATES,)),
         dma((QUAD,)), dma((QUAD,)), dma((QUAD,)), dma((QUAD,)),
@@ -445,19 +473,20 @@
         dma((MATES,)), dma((MATES,)), dma((QUAD,)), dma((QUAD,)),
         dma((QUAD,)), dma((QUAD,)),
     ]
-    query_grad, key_grad, value_grad, router = pl.pallas_call(
+    landed = pl.pallas_call(
         kernel,
         out_shape=(
-            jax.ShapeDtypeStruct((ROWS, HQ * HD), BF16),
-            jax.ShapeDtypeStruct((ROWS, KVH * HD), BF16),
-            jax.ShapeDtypeStruct((ROWS, KVH * HD), BF16),
+            jax.ShapeDtypeStruct((QUAD, ROWS, GROUP * HD), BF16),
+            jax.ShapeDtypeStruct((QUAD, ROWS, 2 * HD), BF16),
+            jax.ShapeDtypeStruct((ROWS, HD), F32),
+            jax.ShapeDtypeStruct((ROWS, HD), F32),
             jax.ShapeDtypeStruct((32, 128), F32),
         ),
-        in_specs=[vmem] * 8,
-        out_specs=(vmem,) * 4,
+        in_specs=[hbm] * 8,
+        out_specs=(vmem,) * 5,
         scratch_shapes=scratch,
         compiler_params=pltpu.CompilerParams(
-            collective_id=0, has_side_effects=True, vmem_limit_bytes=40 * 1024 * 1024
+            collective_id=0, has_side_effects=True, vmem_limit_bytes=63 * 1024 * 1024
         ),
     )(
         queries[0],
@@ -469,6 +498,17 @@
         positions,
         jnp.asarray(rope_rows()),
     )
+    query_grad, key_grad, value_grad, router = pl.pallas_call(
+        finish,
+        out_shape=(
+            jax.ShapeDtypeStruct((ROWS, HQ * HD), BF16),
+            jax.ShapeDtypeStruct((ROWS, KVH * HD), BF16),
+            jax.ShapeDtypeStruct((ROWS, KVH * HD), BF16),
+            jax.ShapeDtypeStruct((32, 128), F32),
+        ),
+        in_specs=[vmem] * 5,
+        out_specs=(vmem,) * 4,
+    )(*landed)
     return (query_grad[None], key_grad[None], value_grad[None], router.reshape(-1))
 
 

time: 77.1 us -> 65.4 us (0.85)
  local copies, waits for them, and re-layouts: 8.16 us -> 0 us
  Pallas kernels: 67.9 us -> 64.6 us
    unnamed x20 -> x0, local copies, waits for them, and re-layouts: 8.16 us -> none
    pallas_call x1 -> x2, Pallas kernels: 67.9 us -> 64.6 us  [the longest x1 62.9 us: shards(): pl.pallas_call(kernel, out_shape=(jax.ShapeDtypeStruct((QUAD, ROWS, GROUP...]
where the time goes in v2:
time: 65.4 us; the launch traced here: 65.2 us
  Pallas kernels  64.6 us (99%)
    pallas_call x1, Pallas kernels, shards(): pl.pallas_call(kernel, out_shape=(jax.ShapeDtypeStruct((QUAD, ROWS, GROUP...  62.9 us
    pallas_call x1, Pallas kernels, shards(): pl.pallas_call(finish, out_shape=(jax.ShapeDtypeStruct((ROWS, HQ * HD), B...  1.75 us

profile of v2, /device:TPU:1, one launch (start us, length us, event | category | flops | bytes accessed | tf_op | source)
XLA Modules:
  0.0 65.2 jit_solution(7596220719169252077)
XLA Ops:
  0.6 62.9 %shard_map.111 = (bf16[4,32,512]{2,1,0:T(8,128)(2,1)}, bf16[4,32,256]{2,1,0:T(8,128)(2,1)}, f32[32,128]{1,0:T(8,128)}, f32[32,128]{1,0:T(8,128)}, f32[32,128]{1,0:T(8,128)}) custom-call(bf16[32,2048]{1,0:T(8,128)(2,1)} %bitcast.11, bf16[32,512]{1,0:T(8,128)(2,1)} %bitcast.13, bf16[32,512]{1,0:T(8,128)(2,1)} %bitcast.14, bf16[32,2048]{1,0:T(8,128)(2,1)} %bitcast.12, ...), custom_call_target="tpu_custom_call" | custom-call | tf_op jit(solution)/shard_map/pallas_call | solution.py:476
  63.5 1.8 %shard_map.112 = (bf16[32,2048]{1,0:T(8,128)(2,1)}, bf16[32,512]{1,0:T(8,128)(2,1)}, bf16[32,512]{1,0:T(8,128)(2,1)}, f32[32,128]{1,0:T(8,128)}) custom-call(bf16[4,32,512]{2,1,0:T(8,128)(2,1)} %get-tuple-element.13.dqr, bf16[4,32,256]{2,1,0:T(8,128)(2,1)} %get-tuple-element.14.kr, f32[32,128]{1,0:T(8,128)} %get-tuple-element.15.cos_s, ...), custom_call_target="tpu_custom_call" | custom-call | tf_op jit(solution)/shard_map/pallas_call | solution.py:501

commit v3 on v2

--- a/solution.py
+++ b/solution.py
@@ -48,11 +48,11 @@
 
 def kernel(
     q_hbm, k_hbm, v_hbm, g_hbm, x_hbm, w_hbm, p_hbm, rope_hbm,
-    dqr, kr, cos_s, sin_s, r4,
+    dqr, kr, cos_s, sin_s, r_sum,
     q_ref, k_ref, v_ref, g_ref, x_ref, w_ref, p_ref, rope_ref, in_sem, gate_s, kv4, qg4, kv, qg, q_s, g_s, s_s, d_s, dqt_s, pb, rb, dqs, cb,
-    ts, tr, rp, r1, r2s, r2, r3s, r3,
+    ts, tr, rz_s, rz, ry_s, ry, rx_s, rx,
     kv_ss, kv_rs, qg_ss, qg_rs, ga_ss, ga_rs, pb_ss, pb_rs, dq_ss, dq_rs, kr_ss, kr_rs,
-    t_ss, t_rs, r1_ss, r1_rs, r2_ss, r2_rs, r3_ss, r3_rs, r4_ss, r4_rs,
+    t_ss, t_rs, rz_ss, rz_rs, ry_ss, ry_rs, rx_ss, rx_rs,
 ):
     dp = lax.axis_index("dp")
     ctx = lax.axis_index("ctx")
@@ -61,6 +61,8 @@
     head = z // 2
     par = z % 2
     mate = run * 2 + par
+    row = run // 2
+    side_x = dp * 2 + run % 2
 
     def quad_at(member):
         return (dp, run * 8 + 2 * member + par)
@@ -68,8 +70,15 @@
     def mate_at(index):
         return (dp, (index // 2) * 8 + 2 * head + index % 2)
 
-    def dp_at(index):
-        return (index, ctx)
+    def z_at(step):
+        return (dp, run * 8 + lax.rem(z + step, 8))
+
+    def y_at(step):
+        return (dp, lax.rem(ctx + 16 * step, 64))
+
+    def x_at(step):
+        to = lax.rem(side_x + step, 8)
+        return (to // 2, (row * 2 + to % 2) * 8 + z)
 
     def remote(src, dst, send, recv, to):
         return pltpu.make_async_remote_copy(
@@ -79,13 +88,14 @@
     def other(step):
         return lax.rem(head + step, QUAD)
 
-    def other_dp(step):
-        return lax.rem(dp + step, 4)
-
     barrier = pltpu.get_barrier_semaphore()
-    for step in range(1, QUAD):
-        pl.semaphore_signal(barrier, inc=1, device_id=quad_at(other(step)), device_id_type=MESH)
-        pl.semaphore_signal(barrier, inc=1, device_id=dp_at(other_dp(step)), device_id_type=MESH)
+
+    def greet_near(step, carry):
+        pl.semaphore_signal(barrier, inc=1, device_id=z_at(step), device_id_type=MESH)
+        pl.semaphore_signal(barrier, inc=1, device_id=x_at(step), device_id_type=MESH)
+        return carry
+
+    lax.fori_loop(1, 8, greet_near, 0)
 
     def greet(step, carry):
         pl.semaphore_signal(
@@ -131,17 +141,37 @@
         kv4[number, :, :HD] = turn(k_ref[:, cols].astype(F32)).astype(BF16)
         kv4[number, :, HD:] = v_ref[:, cols]
 
-    pl.semaphore_wait(barrier, 2 * (QUAD - 1) + MATES - 1)
+    pl.semaphore_wait(barrier, 2 * 7 + MATES - 1)
 
     def kv_copy(step):
         to = other(step)
-        return remote(
-            kv4.at[to], kv.at[mate, pl.ds(head * ROWS, ROWS)], kv_ss.at[step], kv_rs.at[step], quad_at(to)
-        )
+        rows = pl.ds((QUAD - step) * ROWS, ROWS)
+        return remote(kv4.at[to], kv.at[mate, rows], kv_ss.at[step], kv_rs.at[step], quad_at(to))
+
+    def ga_send(part, index):
+        rows = kv.at[mate, pl.ds(part * ROWS, ROWS if part == 0 else 3 * ROWS)]
+        return remote(rows, rows, ga_ss.at[part, index], ga_rs.at[part, mate], mate_at(index))
+
+    def ga_recv(part, index):
+        rows = kv.at[index, pl.ds(part * ROWS, ROWS if part == 0 else 3 * ROWS)]
+        return remote(rows, rows, ga_ss.at[part, index], ga_rs.at[part, index], mate_at(index))
+
+    def ga_start(part):
+        def start(step, carry):
+            index = run * 2 + MATES - 1 - step
+
+            @pl.when(index != mate)
+            def _():
+                ga_send(part, index).start()
+
+            return carry
+
+        lax.fori_loop(run * 2, MATES, start, 0)
 
     for step in range(1, QUAD):
         kv_copy(step).start()
-    kv[mate, pl.ds(pl.multiple_of(head * ROWS, ROWS), ROWS)] = kv4[head]
+    kv[mate, :ROWS] = kv4[head]
+    ga_start(0)
 
     for fetch in fetches[4:]:
         fetch.wait()
@@ -164,21 +194,7 @@
 
     for step in range(1, QUAD):
         kv_copy(step).wait_recv()
-
-    def ga_send(index):
-        return remote(kv.at[mate], kv.at[mate], ga_ss.at[index], ga_rs.at[mate], mate_at(index))
-
-    def ga_recv(index):
-        return remote(kv.at[mate], kv.at[index], ga_ss.at[index], ga_rs.at[index], mate_at(index))
-
-    def ga_start(index, carry):
-        @pl.when(index != mate)
-        def _():
-            ga_send(index).start()
-
-        return carry
-
-    lax.fori_loop(run * 2, MATES, ga_start, 0)
+    ga_start(1)
 
     for step in range(1, QUAD):
         qg_copy(step).wait_recv()
@@ -188,7 +204,7 @@
         g_s[number * SLOT : (number + 1) * SLOT, :] = qg[:, 1, :, cols].reshape(SLOT, HD)
 
     key_at = lax.broadcasted_iota(jnp.int32, (SPAN, QROWS), 0)
-    key_at = (key_at >> 7) * ROWS + ((key_at & 96) << 1) + (key_at & 31)
+    key_at = (key_at >> 7) * ROWS + (((key_at + head * ROWS) & 96) << 1) + (key_at & 31)
     row_at = lax.broadcasted_iota(jnp.int32, (SPAN, QROWS), 1)
     row_at = par * ROWS + ((row_at & 96) << 1) + (row_at & 31)
     ahead = key_at - row_at
@@ -200,7 +216,8 @@
 
             @pl.when(index != mate)
             def _():
-                ga_recv(index).wait_recv()
+                for part in range(2):
+                    ga_recv(part, index).wait_recv()
 
         both = jnp.concatenate([kv[2 * number], kv[2 * number + 1]], axis=0)
         scores = nt(both[:, :HD], q_s[...]) * (SCORE_SCALE * math.log2(math.e))
@@ -277,40 +294,22 @@
     logit_grad = (1.0 - gate_s[:, 0:1]) * term
     part = jnp.sum(logit_grad * x_ref[...].astype(F32), axis=0, keepdims=True)
     for number in range(32):
-        rp[number : number + 1, :] = part[:, number * 128 : (number + 1) * 128]
-
-    own = pl.ds(pl.multiple_of(head * 8, 8), 8)
-
-    def r1_copy(step):
-        to = other(step)
-        rows = pl.ds(pl.multiple_of(to * 8, 8), 8)
-        return remote(rp.at[rows], r1.at[head], r1_ss.at[step], r1_rs.at[step], quad_at(to))
-
-    for step in range(1, QUAD):
-        r1_copy(step).start()
-    r1[head] = rp[own]
+        rz_s[number : number + 1, :] = part[:, number * 128 : (number + 1) * 128]
+
+    def rz_copy(step):
+        return remote(rz_s, rz.at[z], rz_ss.at[step], rz_rs.at[step], z_at(step))
+
+    def ry_copy(step):
+        return remote(ry_s, ry.at[row], ry_ss.at[step], ry_rs.at[step], y_at(step))
+
+    def rx_copy(step):
+        return remote(rx_s, rx.at[side_x], rx_ss.at[step], rx_rs.at[step], x_at(step))
+
+    for step in range(1, 8):
+        rz_copy(step).start()
+    rz[z] = rz_s[...]
 
     lax.fori_loop(half, run + 1, grad_step, 0)
-
-    for step in range(1, QUAD):
-        r1_copy(step).wait_recv()
-    r2s[...] = r1[0] + r1[1] + r1[2] + r1[3]
-
-    def r2_send(index):
-        return remote(r2s, r2.at[mate], r2_ss.at[index], r2_rs.at[mate], mate_at(index))
-
-    def r2_recv(index):
-        return remote(r2s, r2.at[index], r2_ss.at[index], r2_rs.at[index], mate_at(index))
-
-    def r2_start(index, carry):
-        @pl.when(index != mate)
-        def _():
-            r2_send(index).start()
-
-        return carry
-
-    lax.fori_loop(0, MATES, r2_start, 0)
-    r2[mate] = r2s[...]
 
     turned = dqt_s[...].T.astype(BF16)
     for number in range(GROUP):
@@ -334,55 +333,43 @@
 
         return total + rb[index].astype(F32)
 
+    for step in range(1, 8):
+        rz_copy(step).wait_recv()
+    ry_s[...] = sum((rz[number] for number in range(1, 8)), start=rz[0])
+    for step in range(1, 4):
+        ry_copy(step).start()
+    ry[row] = ry_s[...]
+
     middle = run + MATES // 2
     total = lax.fori_loop(run * 2, middle, gather_sum, jnp.zeros((SLOT, 2 * HD), F32))
 
-    def r2_sum(index, total):
-        @pl.when(index != mate)
-        def _():
-            r2_recv(index).wait_recv()
-
-        return total + r2[index]
-
-    r3s[...] = lax.fori_loop(0, MATES, r2_sum, jnp.zeros((8, 128), F32))
-
-    def r3_copy(step):
-        return remote(r3s, r3.at[dp], r3_ss.at[step], r3_rs.at[step], dp_at(other_dp(step)))
-
     for step in range(1, 4):
-        r3_copy(step).start()
-    r3[dp] = r3s[...]
+        ry_copy(step).wait_recv()
+    rx_s[...] = ry[0] + ry[1] + ry[2] + ry[3]
+    for step in range(1, 8):
+        rx_copy(step).start()
+    rx[side_x] = rx_s[...]
 
     total = lax.fori_loop(middle, MATES, gather_sum, total)
     cb[...] = total.astype(BF16)
 
     def kr_copy(step):
-        to = other(step)
-        rows = pl.ds(pl.multiple_of(to * ROWS, ROWS), ROWS)
-        return remote(cb.at[rows], kr.at[head], kr_ss.at[step], kr_rs.at[step], quad_at(to))
+        rows = cb.at[pl.ds(step * ROWS, ROWS)]
+        return remote(rows, kr.at[head], kr_ss.at[step], kr_rs.at[step], quad_at(other(step)))
 
     for step in range(1, QUAD):
         kr_copy(step).start()
-    kr[head] = cb[pl.ds(pl.multiple_of(head * ROWS, ROWS), ROWS)]
-
-    for step in range(1, 4):
-        r3_copy(step).wait_recv()
-    r4[own] = (r3[0] + r3[1] + r3[2] + r3[3]) * (1.0 / math.sqrt(4 * 2048))
-
-    def r4_copy(step):
-        return remote(r4.at[own], r4.at[own], r4_ss.at[step], r4_rs.at[step], quad_at(other(step)))
-
-    for step in range(1, QUAD):
-        r4_copy(step).start()
-
-    for step in range(1, QUAD):
-        for copy in (kv_copy, qg_copy, t_copy, dq_copy, r1_copy, r3_copy):
+    kr[head] = cb[:ROWS]
+
+    for step in range(1, QUAD):
+        for copy in (kv_copy, qg_copy, t_copy, dq_copy, ry_copy):
             copy(step).wait_send()
 
     def drain_late(index, carry):
         @pl.when(index != mate)
         def _():
-            ga_send(index).wait_send()
+            for part in range(2):
+                ga_send(part, index).wait_send()
 
         return carry
 
@@ -397,22 +384,20 @@
 
     lax.fori_loop(0, run * 2 + 2, drain_early, 0)
 
-    def drain_all(index, carry):
-        @pl.when(index != mate)
-        def _():
-            r2_send(index).wait_send()
-
-        return carry
-
-    lax.fori_loop(0, MATES, drain_all, 0)
-    for step in range(1, QUAD):
-        for copy in (dq_copy, kr_copy, r4_copy):
+    for step in range(1, 8):
+        rz_copy(step).wait_send()
+    for step in range(1, 8):
+        rx_copy(step).wait_recv()
+    r_sum[...] = sum((rx[number] for number in range(1, 8)), start=rx[0]) * (1.0 / math.sqrt(4 * 2048))
+    for step in range(1, QUAD):
+        for copy in (dq_copy, kr_copy):
             copy(step).wait_recv()
-        for copy in (kr_copy, r4_copy):
-            copy(step).wait_send()
-
-
-def finish(dqr, kr, cos_s, sin_s, r4, dq_out, dk_out, dv_out, r_out):
+        kr_copy(step).wait_send()
+    for step in range(1, 8):
+        rx_copy(step).wait_send()
+
+
+def finish(dqr, kr, cos_s, sin_s, r_sum, dq_out, dk_out, dv_out, r_out):
     cos = cos_s[...]
     sin = sin_s[...]
 
@@ -427,7 +412,7 @@
         cols = slice(number * HD, (number + 1) * HD)
         dk_out[:, cols] = turn_back(kr[number, :, :HD].astype(F32)).astype(BF16)
         dv_out[:, cols] = kr[number, :, HD:]
-    r_out[...] = r4[...]
+    r_out[...] = r_sum[...]
 
 
 def shards(queries, keys, values, out_grad, routed_inputs, router_weight, positions):
@@ -461,17 +446,16 @@
         pltpu.VMEM((8, 128), F32),
         pltpu.VMEM((QUAD, 8, 128), F32),
         pltpu.VMEM((32, 128), F32),
-        pltpu.VMEM((QUAD, 8, 128), F32),
-        pltpu.VMEM((8, 128), F32),
-        pltpu.VMEM((MATES, 8, 128), F32),
-        pltpu.VMEM((8, 128), F32),
-        pltpu.VMEM((4, 8, 128), F32),
+        pltpu.VMEM((8, 32, 128), F32),
+        pltpu.VMEM((32, 128), F32),
+        pltpu.VMEM((4, 32, 128), F32),
+        pltpu.VMEM((32, 128), F32),
+        pltpu.VMEM((8, 32, 128), F32),
         dma((QUAD,)), dma((QUAD,)), dma((QUAD,)), dma((QUAD,)),
-        dma((MATES,)), dma((MATES,)), dma((MATES,)), dma((MATES,)),
+        dma((QUAD, MATES)), dma((QUAD, MATES)), dma((MATES,)), dma((MATES,)),
         dma((QUAD,)), dma((QUAD,)), dma((QUAD,)), dma((QUAD,)),
-        dma((QUAD,)), dma((QUAD,)), dma((QUAD,)), dma((QUAD,)),
-        dma((MATES,)), dma((MATES,)), dma((QUAD,)), dma((QUAD,)),
-        dma((QUAD,)), dma((QUAD,)),
+        dma((QUAD,)), dma((QUAD,)), dma((8,)), dma((8,)),
+        dma((4,)), dma((4,)), dma((8,)), dma((8,)),
     ]
     landed = pl.pallas_call(
         kernel,

time: 65.4 us -> 55.8 us (0.85)
  Pallas kernels: 64.6 us -> 55 us
    pallas_call x1, Pallas kernels: 62.9 us -> 53.3 us  [shards(): pl.pallas_call(kernel, out_shape=(jax.ShapeDtypeStruct((QUAD, ROWS, GROUP...]
where the time goes in v3:
time: 55.8 us; the launch traced here: 55.7 us
  Pallas kernels  55 us (99%)
  between operations  0.64 us (1%)
    pallas_call x1, Pallas kernels, shards(): pl.pallas_call(kernel, out_shape=(jax.ShapeDtypeStruct((QUAD, ROWS, GROUP...  53.3 us
    pallas_call x1, Pallas kernels, shards(): pl.pallas_call(finish, out_shape=(jax.ShapeDtypeStruct((ROWS, HQ * HD), B...  1.75 us

profile of v3, /device:TPU:1, one launch (start us, length us, event | category | flops | bytes accessed | tf_op | source)
XLA Modules:
  0.0 55.7 jit_solution(2997388214029575689)
XLA Ops:
  0.6 53.3 %shard_map.111 = (bf16[4,32,512]{2,1,0:T(8,128)(2,1)}, bf16[4,32,256]{2,1,0:T(8,128)(2,1)}, f32[32,128]{1,0:T(8,128)}, f32[32,128]{1,0:T(8,128)}, f32[32,128]{1,0:T(8,128)}) custom-call(bf16[32,2048]{1,0:T(8,128)(2,1)} %bitcast.11, bf16[32,512]{1,0:T(8,128)(2,1)} %bitcast.13, bf16[32,512]{1,0:T(8,128)(2,1)} %bitcast.14, bf16[32,2048]{1,0:T(8,128)(2,1)} %bitcast.12, ...), custom_call_target="tpu_custom_call" | custom-call | tf_op jit(solution)/shard_map/pallas_call | solution.py:460
  53.9 1.8 %shard_map.112 = (bf16[32,2048]{1,0:T(8,128)(2,1)}, bf16[32,512]{1,0:T(8,128)(2,1)}, bf16[32,512]{1,0:T(8,128)(2,1)}, f32[32,128]{1,0:T(8,128)}) custom-call(bf16[4,32,512]{2,1,0:T(8,128)(2,1)} %get-tuple-element.13.dqr, bf16[4,32,256]{2,1,0:T(8,128)(2,1)} %get-tuple-element.14.kr, f32[32,128]{1,0:T(8,128)} %get-tuple-element.15.cos_s, ...), custom_call_target="tpu_custom_call" | custom-call | tf_op jit(solution)/shard_map/pallas_call | solution.py:485

commit v4 on v3

--- a/solution.py
+++ b/solution.py
@@ -85,25 +85,11 @@
             src_ref=src, dst_ref=dst, send_sem=send, recv_sem=recv, device_id=to, device_id_type=MESH
         )
 
+    def settle(ref, sem):
+        pltpu.make_async_copy(ref, ref, sem).wait()
+
     def other(step):
         return lax.rem(head + step, QUAD)
-
-    barrier = pltpu.get_barrier_semaphore()
-
-    def greet_near(step, carry):
-        pl.semaphore_signal(barrier, inc=1, device_id=z_at(step), device_id_type=MESH)
-        pl.semaphore_signal(barrier, inc=1, device_id=x_at(step), device_id_type=MESH)
-        return carry
-
-    lax.fori_loop(1, 8, greet_near, 0)
-
-    def greet(step, carry):
-        pl.semaphore_signal(
-            barrier, inc=1, device_id=mate_at(lax.rem(mate + step, MATES)), device_id_type=MESH
-        )
-        return carry
-
-    lax.fori_loop(1, MATES, greet, 0)
 
     pairs = (
         (p_hbm, p_ref), (rope_hbm, rope_ref), (k_hbm, k_ref), (v_hbm, v_ref),
@@ -114,6 +100,24 @@
     ]
     for fetch in fetches:
         fetch.start()
+
+    barrier = pltpu.get_barrier_semaphore()
+
+    def greet_near(step, carry):
+        pl.semaphore_signal(barrier, inc=1, device_id=z_at(step), device_id_type=MESH)
+        pl.semaphore_signal(barrier, inc=1, device_id=x_at(step), device_id_type=MESH)
+        return carry
+
+    lax.fori_loop(1, 8, greet_near, 0)
+
+    def greet(step, carry):
+        pl.semaphore_signal(
+            barrier, inc=1, device_id=mate_at(lax.rem(mate + step, MATES)), device_id_type=MESH
+        )
+        return carry
+
+    lax.fori_loop(1, MATES, greet, 0)
+
     fetches[0].wait()
     fetches[1].wait()
 
@@ -146,15 +150,11 @@
     def kv_copy(step):
         to = other(step)
         rows = pl.ds((QUAD - step) * ROWS, ROWS)
-        return remote(kv4.at[to], kv.at[mate, rows], kv_ss.at[step], kv_rs.at[step], quad_at(to))
+        return remote(kv4.at[to], kv.at[mate, rows], kv_ss.at[0], kv_rs.at[0], quad_at(to))
 
     def ga_send(part, index):
         rows = kv.at[mate, pl.ds(part * ROWS, ROWS if part == 0 else 3 * ROWS)]
-        return remote(rows, rows, ga_ss.at[part, index], ga_rs.at[part, mate], mate_at(index))
-
-    def ga_recv(part, index):
-        rows = kv.at[index, pl.ds(part * ROWS, ROWS if part == 0 else 3 * ROWS)]
-        return remote(rows, rows, ga_ss.at[part, index], ga_rs.at[part, index], mate_at(index))
+        return remote(rows, rows, ga_ss.at[0], ga_rs.at[run], mate_at(index))
 
     def ga_start(part):
         def start(step, carry):
@@ -186,18 +186,16 @@
 
     def qg_copy(step):
         to = other(step)
-        return remote(qg4.at[to], qg.at[head], qg_ss.at[step], qg_rs.at[step], quad_at(to))
+        return remote(qg4.at[to], qg.at[head], qg_ss.at[0], qg_rs.at[0], quad_at(to))
 
     for step in range(1, QUAD):
         qg_copy(step).start()
     qg[head] = qg4[head]
 
-    for step in range(1, QUAD):
-        kv_copy(step).wait_recv()
+    settle(kv4.at[pl.ds(0, 3)], kv_rs.at[0])
     ga_start(1)
 
-    for step in range(1, QUAD):
-        qg_copy(step).wait_recv()
+    settle(qg.at[pl.ds(0, 3)], qg_rs.at[0])
     for number in range(GROUP):
         cols = slice(number * HD, (number + 1) * HD)
         q_s[number * SLOT : (number + 1) * SLOT, :] = qg[:, 0, :, cols].reshape(SLOT, HD)
@@ -211,13 +209,14 @@
 
     def score_step(back, top):
         number = run - back
-        for side in range(2):
-            index = 2 * number + side
-
-            @pl.when(index != mate)
-            def _():
-                for part in range(2):
-                    ga_recv(part, index).wait_recv()
+
+        @pl.when(number != run)
+        def _():
+            settle(kv.at[pl.ds(0, 2)], ga_rs.at[number])
+
+        @pl.when(number == run)
+        def _():
+            settle(kv.at[0], ga_rs.at[number])
 
         both = jnp.concatenate([kv[2 * number], kv[2 * number + 1]], axis=0)
         scores = nt(both[:, :HD], q_s[...]) * (SCORE_SCALE * math.log2(math.e))
@@ -248,17 +247,14 @@
     ts[...] = jnp.broadcast_to(term * math.sqrt(HD), (8, SLOT))
 
     def t_copy(step):
-        return remote(ts, tr.at[head], t_ss.at[step], t_rs.at[step], quad_at(other(step)))
+        return remote(ts, tr.at[head], t_ss.at[0], t_rs.at[0], quad_at(other(step)))
 
     for step in range(1, QUAD):
         t_copy(step).start()
     tr[head] = ts[...]
 
     def pb_send(index):
-        return remote(pb.at[index], rb.at[mate], pb_ss.at[index], pb_rs.at[mate], mate_at(index))
-
-    def pb_recv(index):
-        return remote(pb.at[index], rb.at[index], pb_ss.at[index], pb_rs.at[index], mate_at(index))
+        return remote(pb.at[index], rb.at[mate], pb_ss.at[0], pb_rs.at[run], mate_at(index))
 
     dqt_s[...] = jnp.zeros_like(dqt_s)
 
@@ -284,8 +280,7 @@
     half = (run + 1) // 2
     lax.fori_loop(0, half, grad_step, 0)
 
-    for step in range(1, QUAD):
-        t_copy(step).wait_recv()
+    settle(tr.at[pl.ds(0, 3)], t_rs.at[0])
     term = tr[0] + tr[1] + tr[2] + tr[3]
     spot = lax.broadcasted_iota(jnp.int32, (ROWS, SLOT), 0) + head * ROWS
     pick = lax.broadcasted_iota(jnp.int32, (ROWS, SLOT), 1) == spot
@@ -297,13 +292,13 @@
         rz_s[number : number + 1, :] = part[:, number * 128 : (number + 1) * 128]
 
     def rz_copy(step):
-        return remote(rz_s, rz.at[z], rz_ss.at[step], rz_rs.at[step], z_at(step))
+        return remote(rz_s, rz.at[z], rz_ss.at[0], rz_rs.at[0], z_at(step))
 
     def ry_copy(step):
-        return remote(ry_s, ry.at[row], ry_ss.at[step], ry_rs.at[step], y_at(step))
+        return remote(ry_s, ry.at[row], ry_ss.at[0], ry_rs.at[0], y_at(step))
 
     def rx_copy(step):
-        return remote(rx_s, rx.at[side_x], rx_ss.at[step], rx_rs.at[step], x_at(step))
+        return remote(rx_s, rx.at[side_x], rx_ss.at[0], rx_rs.at[0], x_at(step))
 
     for step in range(1, 8):
         rz_copy(step).start()
@@ -318,7 +313,7 @@
 
     def dq_copy(step):
         to = other(step)
-        return remote(dqs.at[to], dqr.at[head], dq_ss.at[step], dq_rs.at[step], quad_at(to))
+        return remote(dqs.at[to], dqr.at[head], dq_ss.at[0], dq_rs.at[0], quad_at(to))
 
     for step in range(1, QUAD):
         dq_copy(step).start()
@@ -326,75 +321,68 @@
 
     rb[mate] = pb[mate]
 
-    def gather_sum(index, total):
-        @pl.when(index != mate)
+    def gather_sum(number, total):
+        @pl.when(number != run)
         def _():
-            pb_recv(index).wait_recv()
-
-        return total + rb[index].astype(F32)
-
-    for step in range(1, 8):
-        rz_copy(step).wait_recv()
+            settle(rb.at[pl.ds(0, 2)], pb_rs.at[number])
+
+        @pl.when(number == run)
+        def _():
+            settle(rb.at[0], pb_rs.at[number])
+
+        return total + (rb[2 * number].astype(F32) + rb[2 * number + 1].astype(F32))
+
+    settle(rz.at[pl.ds(0, 7)], rz_rs.at[0])
     ry_s[...] = sum((rz[number] for number in range(1, 8)), start=rz[0])
     for step in range(1, 4):
         ry_copy(step).start()
     ry[row] = ry_s[...]
 
-    middle = run + MATES // 2
-    total = lax.fori_loop(run * 2, middle, gather_sum, jnp.zeros((SLOT, 2 * HD), F32))
-
-    for step in range(1, 4):
-        ry_copy(step).wait_recv()
+    middle = (run + SUPER) // 2
+    total = lax.fori_loop(run, middle, gather_sum, jnp.zeros((SLOT, 2 * HD), F32))
+
+    settle(ry.at[pl.ds(0, 3)], ry_rs.at[0])
     rx_s[...] = ry[0] + ry[1] + ry[2] + ry[3]
     for step in range(1, 8):
         rx_copy(step).start()
     rx[side_x] = rx_s[...]
 
-    total = lax.fori_loop(middle, MATES, gather_sum, total)
+    total = lax.fori_loop(middle, SUPER, gather_sum, total)
     cb[...] = total.astype(BF16)
 
     def kr_copy(step):
         rows = cb.at[pl.ds(step * ROWS, ROWS)]
-        return remote(rows, kr.at[head], kr_ss.at[step], kr_rs.at[step], quad_at(other(step)))
+        return remote(rows, kr.at[head], kr_ss.at[0], kr_rs.at[0], quad_at(other(step)))
 
     for step in range(1, QUAD):
         kr_copy(step).start()
     kr[head] = cb[:ROWS]
 
-    for step in range(1, QUAD):
-        for copy in (kv_copy, qg_copy, t_copy, dq_copy, ry_copy):
-            copy(step).wait_send()
-
-    def drain_late(index, carry):
-        @pl.when(index != mate)
-        def _():
-            for part in range(2):
-                ga_send(part, index).wait_send()
-
+    settle(kv4.at[pl.ds(0, 3)], kv_ss.at[0])
+    settle(qg.at[pl.ds(0, 3)], qg_ss.at[0])
+    settle(tr.at[pl.ds(0, 3)], t_ss.at[0])
+    settle(dqr.at[pl.ds(0, 3)], dq_ss.at[0])
+    settle(rz.at[pl.ds(0, 7)], rz_ss.at[0])
+    settle(ry.at[pl.ds(0, 3)], ry_ss.at[0])
+    settle(kv.at[0], ga_ss.at[0])
+    settle(pb.at[0], pb_ss.at[0])
+
+    def drain_late(number, carry):
+        settle(kv.at[pl.ds(0, 2)], ga_ss.at[0])
         return carry
 
-    lax.fori_loop(run * 2, MATES, drain_late, 0)
-
-    def drain_early(index, carry):
-        @pl.when(index != mate)
-        def _():
-            pb_send(index).wait_send()
-
+    def drain_early(number, carry):
+        settle(pb.at[pl.ds(0, 2)], pb_ss.at[0])
         return carry
 
-    lax.fori_loop(0, run * 2 + 2, drain_early, 0)
-
-    for step in range(1, 8):
-        rz_copy(step).wait_send()
-    for step in range(1, 8):
-        rx_copy(step).wait_recv()
+    lax.fori_loop(run + 1, SUPER, drain_late, 0)
+    lax.fori_loop(0, run, drain_early, 0)
+    settle(rx.at[pl.ds(0, 7)], rx_rs.at[0])
     r_sum[...] = sum((rx[number] for number in range(1, 8)), start=rx[0]) * (1.0 / math.sqrt(4 * 2048))
-    for step in range(1, QUAD):
-        for copy in (dq_copy, kr_copy):
-            copy(step).wait_recv()
-        kr_copy(step).wait_send()
-    for step in range(1, 8):
-        rx_copy(step).wait_send()
+    settle(dqr.at[pl.ds(0, 3)], dq_rs.at[0])
+    settle(kr.at[pl.ds(0, 3)], kr_rs.at[0])
+    settle(kr.at[pl.ds(0, 3)], kr_ss.at[0])
+    settle(rx.at[pl.ds(0, 7)], rx_ss.at[0])
 
 
 def finish(dqr, kr, cos_s, sin_s, r_sum, dq_out, dk_out, dv_out, r_out):
@@ -451,11 +439,11 @@
         pltpu.VMEM((4, 32, 128), F32),
         pltpu.VMEM((32, 128), F32),
         pltpu.VMEM((8, 32, 128), F32),
-        dma((QUAD,)), dma((QUAD,)), dma((QUAD,)), dma((QUAD,)),
-        dma((QUAD, MATES)), dma((QUAD, MATES)), dma((MATES,)), dma((MATES,)),
-        dma((QUAD,)), dma((QUAD,)), dma((QUAD,)), dma((QUAD,)),
-        dma((QUAD,)), dma((QUAD,)), dma((8,)), dma((8,)),
-        dma((4,)), dma((4,)), dma((8,)), dma((8,)),
+        dma((1,)), dma((1,)), dma((1,)), dma((1,)),
+        dma((1,)), dma((SUPER,)), dma((1,)), dma((SUPER,)),
+        dma((1,)), dma((1,)), dma((1,)), dma((1,)),
+        dma((1,)), dma((1,)), dma((1,)), dma((1,)),
+        dma((1,)), dma((1,)), dma((1,)), dma((1,)),
     ]
     landed = pl.pallas_call(
         kernel,

time: 55.8 us -> 53.6 us (0.961)
  Pallas kernels: 55 us -> 52.8 us
    pallas_call x1, Pallas kernels: 53.3 us -> 51.1 us  [shards(): pl.pallas_call(kernel, out_shape=(jax.ShapeDtypeStruct((QUAD, ROWS, GROUP...]
where the time goes in v4:
time: 53.6 us; the launch traced here: 53.5 us
  Pallas kernels  52.8 us (99%)
  between operations  0.64 us (1%)
    pallas_call x1, Pallas kernels, shards(): pl.pallas_call(kernel, out_shape=(jax.ShapeDtypeStruct((QUAD, ROWS, GROUP...  51.1 us
    pallas_call x1, Pallas kernels, shards(): pl.pallas_call(finish, out_shape=(jax.ShapeDtypeStruct((ROWS, HQ * HD), B...  1.75 us

profile of v4, /device:TPU:1, one launch (start us, length us, event | category | flops | bytes accessed | tf_op | source)
XLA Modules:
  0.0 53.5 jit_solution(10515733671458925966)
XLA Ops:
  0.6 51.1 %shard_map.111 = (bf16[4,32,512]{2,1,0:T(8,128)(2,1)}, bf16[4,32,256]{2,1,0:T(8,128)(2,1)}, f32[32,128]{1,0:T(8,128)}, f32[32,128]{1,0:T(8,128)}, f32[32,128]{1,0:T(8,128)}) custom-call(bf16[32,2048]{1,0:T(8,128)(2,1)} %bitcast.11, bf16[32,512]{1,0:T(8,128)(2,1)} %bitcast.13, bf16[32,512]{1,0:T(8,128)(2,1)} %bitcast.14, bf16[32,2048]{1,0:T(8,128)(2,1)} %bitcast.12, ...), custom_call_target="tpu_custom_call" | custom-call | tf_op jit(solution)/shard_map/pallas_call | solution.py:448
  51.7 1.8 %shard_map.112 = (bf16[32,2048]{1,0:T(8,128)(2,1)}, bf16[32,512]{1,0:T(8,128)(2,1)}, bf16[32,512]{1,0:T(8,128)(2,1)}, f32[32,128]{1,0:T(8,128)}) custom-call(bf16[4,32,512]{2,1,0:T(8,128)(2,1)} %get-tuple-element.13.dqr, bf16[4,32,256]{2,1,0:T(8,128)(2,1)} %get-tuple-element.14.kr, f32[32,128]{1,0:T(8,128)} %get-tuple-element.15.cos_s, ...), custom_call_target="tpu_custom_call" | custom-call | tf_op jit(solution)/shard_map/pallas_call | solution.py:473

commit v5 on v4

--- a/solution.py
+++ b/solution.py
@@ -88,6 +88,9 @@
     def settle(ref, sem):
         pltpu.make_async_copy(ref, ref, sem).wait()
 
+    def ring_sum(slots, count):
+        return sum((slots[number].astype(F32) for number in range(1, count)), start=slots[0].astype(F32))
+
     def other(step):
         return lax.rem(head + step, QUAD)
 
@@ -103,20 +106,12 @@
 
     barrier = pltpu.get_barrier_semaphore()
 
-    def greet_near(step, carry):
+    for step in range(1, 8):
         pl.semaphore_signal(barrier, inc=1, device_id=z_at(step), device_id_type=MESH)
         pl.semaphore_signal(barrier, inc=1, device_id=x_at(step), device_id_type=MESH)
-        return carry
-
-    lax.fori_loop(1, 8, greet_near, 0)
-
-    def greet(step, carry):
-        pl.semaphore_signal(
-            barrier, inc=1, device_id=mate_at(lax.rem(mate + step, MATES)), device_id_type=MESH
-        )
-        return carry
-
-    lax.fori_loop(1, MATES, greet, 0)
+    for step in range(1, MATES):
+        to = mate_at(lax.rem(mate + step, MATES))
+        pl.semaphore_signal(barrier, inc=1, device_id=to, device_id_type=MESH)
 
     fetches[0].wait()
     fetches[1].wait()
@@ -157,16 +152,14 @@
         return remote(rows, rows, ga_ss.at[0], ga_rs.at[run], mate_at(index))
 
     def ga_start(part):
-        def start(step, carry):
-            index = run * 2 + MATES - 1 - step
-
-            @pl.when(index != mate)
+        for number in reversed(range(1, SUPER)):
+
+            @pl.when(number > run)
             def _():
-                ga_send(part, index).start()
-
-            return carry
-
-        lax.fori_loop(run * 2, MATES, start, 0)
+                ga_send(part, 2 * number).start()
+                ga_send(part, 2 * number + 1).start()
+
+        ga_send(part, run * 2 + 1 - par).start()
 
     for step in range(1, QUAD):
         kv_copy(step).start()
@@ -207,7 +200,8 @@
     row_at = par * ROWS + ((row_at & 96) << 1) + (row_at & 31)
     ahead = key_at - row_at
 
-    def score_step(back, top):
+    def score_step(back, carry):
+        top, mass, pull = carry
         number = run - back
 
         @pl.when(number != run)
@@ -222,24 +216,23 @@
         scores = nt(both[:, :HD], q_s[...]) * (SCORE_SCALE * math.log2(math.e))
         scores = jnp.where(ahead <= (run - number) * SPAN, scores, NEG)
         s_s[number] = scores
-        d_s[number] = nt(both[:, HD:], g_s[...]) * SCORE_SCALE
-        return jnp.maximum(top, jnp.max(scores, axis=0, keepdims=True))
-
-    top = lax.fori_loop(0, run + 1, score_step, jnp.full((1, QROWS), NEG, F32))
-
-    def mass_step(number, carry):
-        mass, pull = carry
-        raised = jnp.exp2(s_s[number] - top)
-        s_s[number] = raised
+        slopes = nt(both[:, HD:], g_s[...]) * SCORE_SCALE
+        d_s[number] = slopes
+        higher = jnp.maximum(top, jnp.max(scores, axis=0, keepdims=True))
+        fade = jnp.exp2(top - higher)
+        raised = jnp.exp2(scores - higher)
         return (
-            mass + jnp.sum(raised, axis=0, keepdims=True),
-            pull + jnp.sum(raised * d_s[number], axis=0, keepdims=True),
+            higher,
+            mass * fade + jnp.sum(raised, axis=0, keepdims=True),
+            pull * fade + jnp.sum(raised * slopes, axis=0, keepdims=True),
         )
 
     zero_row = jnp.zeros((1, QROWS), F32)
-    mass, pull = lax.fori_loop(0, run + 1, mass_step, (zero_row, zero_row))
-    inverse = 1.0 / mass
-    delta = pull * inverse
+    lowest = jnp.full((1, QROWS), NEG, F32)
+    top, mass, pull = lax.fori_loop(0, run + 1, score_step, (lowest, zero_row, zero_row))
+
+    level = top + jnp.log2(mass)
+    delta = pull / mass
 
     term = delta[:, :SLOT]
     for number in range(1, GROUP):
@@ -259,7 +252,7 @@
     dqt_s[...] = jnp.zeros_like(dqt_s)
 
     def grad_step(number, carry):
-        weights = s_s[number] * inverse
+        weights = jnp.exp2(s_s[number] - level)
         probs = weights.astype(BF16)
         slope = (weights * (d_s[number] - delta)).astype(BF16)
         keys = jnp.concatenate([kv[2 * number, :, :HD], kv[2 * number + 1, :, :HD]], axis=0)
@@ -288,8 +281,8 @@
     term = jnp.sum(jnp.where(pick, term, 0.0), axis=1, keepdims=True)
     logit_grad = (1.0 - gate_s[:, 0:1]) * term
     part = jnp.sum(logit_grad * x_ref[...].astype(F32), axis=0, keepdims=True)
-    for number in range(32):
-        rz_s[number : number + 1, :] = part[:, number * 128 : (number + 1) * 128]
+    part = jnp.concatenate([part[:, number * 128 : (number + 1) * 128] for number in range(32)], axis=0)
+    rz_s[...] = part.astype(BF16)
 
     def rz_copy(step):
         return remote(rz_s, rz.at[z], rz_ss.at[0], rz_rs.at[0], z_at(step))
@@ -333,7 +326,7 @@
         return total + (rb[2 * number].astype(F32) + rb[2 * number + 1].astype(F32))
 
     settle(rz.at[pl.ds(0, 7)], rz_rs.at[0])
-    ry_s[...] = sum((rz[number] for number in range(1, 8)), start=rz[0])
+    ry_s[...] = ring_sum(rz, 8).astype(BF16)
     for step in range(1, 4):
         ry_copy(step).start()
     ry[row] = ry_s[...]
@@ -342,7 +335,7 @@
     total = lax.fori_loop(run, middle, gather_sum, jnp.zeros((SLOT, 2 * HD), F32))
 
     settle(ry.at[pl.ds(0, 3)], ry_rs.at[0])
-    rx_s[...] = ry[0] + ry[1] + ry[2] + ry[3]
+    rx_s[...] = ring_sum(ry, 4).astype(BF16)
     for step in range(1, 8):
         rx_copy(step).start()
     rx[side_x] = rx_s[...]
@@ -378,7 +371,7 @@
     lax.fori_loop(run + 1, SUPER, drain_late, 0)
     lax.fori_loop(0, run, drain_early, 0)
     settle(rx.at[pl.ds(0, 7)], rx_rs.at[0])
-    r_sum[...] = sum((rx[number] for number in range(1, 8)), start=rx[0]) * (1.0 / math.sqrt(4 * 2048))
+    r_sum[...] = ring_sum(rx, 8) * (1.0 / math.sqrt(4 * 2048))
     settle(dqr.at[pl.ds(0, 3)], dq_rs.at[0])
     settle(kr.at[pl.ds(0, 3)], kr_rs.at[0])
     settle(kr.at[pl.ds(0, 3)], kr_ss.at[0])
@@ -433,12 +426,12 @@
         pltpu.VMEM((SLOT, 2 * HD), BF16),
         pltpu.VMEM((8, 128), F32),
         pltpu.VMEM((QUAD, 8, 128), F32),
-        pltpu.VMEM((32, 128), F32),
-        pltpu.VMEM((8, 32, 128), F32),
-        pltpu.VMEM((32, 128), F32),
-        pltpu.VMEM((4, 32, 128), F32),
-        pltpu.VMEM((32, 128), F32),
-        pltpu.VMEM((8, 32, 128), F32),
+        pltpu.VMEM((32, 128), BF16),
+        pltpu.VMEM((8, 32, 128), BF16),
+        pltpu.VMEM((32, 128), BF16),
+        pltpu.VMEM((4, 32, 128), BF16),
+        pltpu.VMEM((32, 128), BF16),
+        pltpu.VMEM((8, 32, 128), BF16),
         dma((1,)), dma((1,)), dma((1,)), dma((1,)),
         dma((1,)), dma((SUPER,)), dma((1,)), dma((SUPER,)),
         dma((1,)), dma((1,)), dma((1,)), dma((1,)),

time: 53.6 us -> 52.3 us (0.976)
  the two profiles are of different devices: /device:TPU:1 before, /device:TPU:8 now
where the time goes in v5:
time: 52.3 us; the launch traced here: 52.2 us
  Pallas kernels  51.6 us (99%)
  between operations  0.64 us (1%)
    pallas_call x1, Pallas kernels, shards(): pl.pallas_call(kernel, out_shape=(jax.ShapeDtypeStruct((QUAD, ROWS, GROUP...  49.8 us
    pallas_call x1, Pallas kernels, shards(): pl.pallas_call(finish, out_shape=(jax.ShapeDtypeStruct((ROWS, HQ * HD), B...  1.75 us

profile of v5, /device:TPU:8, one launch (start us, length us, event | category | flops | bytes accessed | tf_op | source)
XLA Modules:
  0.0 52.2 jit_solution(8544629002334603804)
XLA Ops:
  0.6 49.8 %shard_map.111 = (bf16[4,32,512]{2,1,0:T(8,128)(2,1)}, bf16[4,32,256]{2,1,0:T(8,128)(2,1)}, f32[32,128]{1,0:T(8,128)}, f32[32,128]{1,0:T(8,128)}, f32[32,128]{1,0:T(8,128)}) custom-call(bf16[32,2048]{1,0:T(8,128)(2,1)} %bitcast.11, bf16[32,512]{1,0:T(8,128)(2,1)} %bitcast.13, bf16[32,512]{1,0:T(8,128)(2,1)} %bitcast.14, bf16[32,2048]{1,0:T(8,128)(2,1)} %bitcast.12, ...), custom_call_target="tpu_custom_call" | custom-call | tf_op jit(solution)/shard_map/pallas_call | solution.py:441
  50.5 1.8 %shard_map.112 = (bf16[32,2048]{1,0:T(8,128)(2,1)}, bf16[32,512]{1,0:T(8,128)(2,1)}, bf16[32,512]{1,0:T(8,128)(2,1)}, f32[32,128]{1,0:T(8,128)}) custom-call(bf16[4,32,512]{2,1,0:T(8,128)(2,1)} %get-tuple-element.13.dqr, bf16[4,32,256]{2,1,0:T(8,128)(2,1)} %get-tuple-element.14.kr, f32[32,128]{1,0:T(8,128)} %get-tuple-element.15.cos_s, ...), custom_call_target="tpu_custom_call" | custom-call | tf_op jit(solution)/shard_map/pallas_call | solution.py:466

commit v6 on v5

--- a/solution.py
+++ b/solution.py
@@ -61,8 +61,8 @@
     head = z // 2
     par = z % 2
     mate = run * 2 + par
-    row = run // 2
-    side_x = dp * 2 + run % 2
+    core = dp % 2
+    spot_xy = run * 2 + dp // 2
 
     def quad_at(member):
         return (dp, run * 8 + 2 * member + par)
@@ -73,12 +73,11 @@
     def z_at(step):
         return (dp, run * 8 + lax.rem(z + step, 8))
 
-    def y_at(step):
-        return (dp, lax.rem(ctx + 16 * step, 64))
-
-    def x_at(step):
-        to = lax.rem(side_x + step, 8)
-        return (to // 2, (row * 2 + to % 2) * 8 + z)
+    def xy_at(step):
+        to = lax.rem(spot_xy + step, 16)
+        return (to % 2 * 2 + core, to // 2 * 8 + z)
+
+    twin = (dp + 1 - 2 * core, ctx)
 
     def remote(src, dst, send, recv, to):
         return pltpu.make_async_remote_copy(
@@ -106,11 +105,13 @@
 
     barrier = pltpu.get_barrier_semaphore()
 
+    pl.semaphore_signal(barrier, inc=1, device_id=twin, device_id_type=MESH)
     for step in range(1, 8):
         pl.semaphore_signal(barrier, inc=1, device_id=z_at(step), device_id_type=MESH)
-        pl.semaphore_signal(barrier, inc=1, device_id=x_at(step), device_id_type=MESH)
-    for step in range(1, MATES):
-        to = mate_at(lax.rem(mate + step, MATES))
+    for step in range(1, 16):
+        pl.semaphore_signal(barrier, inc=1, device_id=xy_at(step), device_id_type=MESH)
+    for step in range(1, SUPER):
+        to = mate_at(lax.rem(run + step, SUPER) * 2 + 1 - par)
         pl.semaphore_signal(barrier, inc=1, device_id=to, device_id_type=MESH)
 
     fetches[0].wait()
@@ -140,7 +141,7 @@
         kv4[number, :, :HD] = turn(k_ref[:, cols].astype(F32)).astype(BF16)
         kv4[number, :, HD:] = v_ref[:, cols]
 
-    pl.semaphore_wait(barrier, 2 * 7 + MATES - 1)
+    pl.semaphore_wait(barrier, 1 + 7 + 15 + SUPER - 1)
 
     def kv_copy(step):
         to = other(step)
@@ -288,10 +289,9 @@
         return remote(rz_s, rz.at[z], rz_ss.at[0], rz_rs.at[0], z_at(step))
 
     def ry_copy(step):
-        return remote(ry_s, ry.at[row], ry_ss.at[0], ry_rs.at[0], y_at(step))
-
-    def rx_copy(step):
-        return remote(rx_s, rx.at[side_x], rx_ss.at[0], rx_rs.at[0], x_at(step))
+        return remote(ry_s, ry.at[spot_xy], ry_ss.at[0], ry_rs.at[0], xy_at(step))
+
+    swap = remote(rx_s, rx.at[core], rx_ss.at[0], rx_rs.at[0], twin)
 
     for step in range(1, 8):
         rz_copy(step).start()
@@ -327,20 +327,11 @@
 
     settle(rz.at[pl.ds(0, 7)], rz_rs.at[0])
     ry_s[...] = ring_sum(rz, 8).astype(BF16)
-    for step in range(1, 4):
+    for step in range(1, 16):
         ry_copy(step).start()
-    ry[row] = ry_s[...]
-
-    middle = (run + SUPER) // 2
-    total = lax.fori_loop(run, middle, gather_sum, jnp.zeros((SLOT, 2 * HD), F32))
-
-    settle(ry.at[pl.ds(0, 3)], ry_rs.at[0])
-    rx_s[...] = ring_sum(ry, 4).astype(BF16)
-    for step in range(1, 8):
-        rx_copy(step).start()
-    rx[side_x] = rx_s[...]
-
-    total = lax.fori_loop(middle, SUPER, gather_sum, total)
+    ry[spot_xy] = ry_s[...]
+
+    total = lax.fori_loop(run, SUPER, gather_sum, jnp.zeros((SLOT, 2 * HD), F32))
     cb[...] = total.astype(BF16)
 
     def kr_copy(step):
@@ -350,13 +341,18 @@
     for step in range(1, QUAD):
         kr_copy(step).start()
     kr[head] = cb[:ROWS]
+
+    settle(ry.at[pl.ds(0, 15)], ry_rs.at[0])
+    rx_s[...] = ring_sum(ry, 16).astype(BF16)
+    swap.start()
+    rx[core] = rx_s[...]
 
     settle(kv4.at[pl.ds(0, 3)], kv_ss.at[0])
     settle(qg.at[pl.ds(0, 3)], qg_ss.at[0])
     settle(tr.at[pl.ds(0, 3)], t_ss.at[0])
     settle(dqr.at[pl.ds(0, 3)], dq_ss.at[0])
     settle(rz.at[pl.ds(0, 7)], rz_ss.at[0])
-    settle(ry.at[pl.ds(0, 3)], ry_ss.at[0])
+    settle(ry.at[pl.ds(0, 15)], ry_ss.at[0])
     settle(kv.at[0], ga_ss.at[0])
     settle(pb.at[0], pb_ss.at[0])
 
@@ -370,12 +366,11 @@
 
     lax.fori_loop(run + 1, SUPER, drain_late, 0)
     lax.fori_loop(0, run, drain_early, 0)
-    settle(rx.at[pl.ds(0, 7)], rx_rs.at[0])
-    r_sum[...] = ring_sum(rx, 8) * (1.0 / math.sqrt(4 * 2048))
+    swap.wait()
+    r_sum[...] = ring_sum(rx, 2) * (1.0 / math.sqrt(4 * 2048))
     settle(dqr.at[pl.ds(0, 3)], dq_rs.at[0])
     settle(kr.at[pl.ds(0, 3)], kr_rs.at[0])
     settle(kr.at[pl.ds(0, 3)], kr_ss.at[0])
-    settle(rx.at[pl.ds(0, 7)], rx_ss.at[0])
 
 
 def finish(dqr, kr, cos_s, sin_s, r_sum, dq_out, dk_out, dv_out, r_out):
@@ -429,9 +424,9 @@
         pltpu.VMEM((32, 128), BF16),
         pltpu.VMEM((8, 32, 128), BF16),
         pltpu.VMEM((32, 128), BF16),
-        pltpu.VMEM((4, 32, 128), BF16),
+        pltpu.VMEM((16, 32, 128), BF16),
         pltpu.VMEM((32, 128), BF16),
-        pltpu.VMEM((8, 32, 128), BF16),
+        pltpu.VMEM((2, 32, 128), BF16),
         dma((1,)), dma((1,)), dma((1,)), dma((1,)),
         dma((1,)), dma((SUPER,)), dma((1,)), dma((SUPER,)),
         dma((1,)), dma((1,)), dma((1,)), dma((1,)),

time: 52.3 us -> 50.8 us (0.971)
  the two profiles are of different devices: /device:TPU:8 before, /device:TPU:1 now
where the time goes in v6:
time: 50.8 us; the launch traced here: 50 us
  Pallas kernels  49.4 us (97%)
  between operations  0.64 us (1%)
    pallas_call x1, Pallas kernels, shards(): pl.pallas_call(kernel, out_shape=(jax.ShapeDtypeStruct((QUAD, ROWS, GROUP...  47.6 us
    pallas_call x1, Pallas kernels, shards(): pl.pallas_call(finish, out_shape=(jax.ShapeDtypeStruct((ROWS, HQ * HD), B...  1.75 us

profile of v6, /device:TPU:1, one launch (start us, length us, event | category | flops | bytes accessed | tf_op | source)
XLA Modules:
  0.0 50.0 jit_solution(13751546696926973939)
XLA Ops:
  0.6 47.6 %shard_map.111 = (bf16[4,32,512]{2,1,0:T(8,128)(2,1)}, bf16[4,32,256]{2,1,0:T(8,128)(2,1)}, f32[32,128]{1,0:T(8,128)}, f32[32,128]{1,0:T(8,128)}, f32[32,128]{1,0:T(8,128)}) custom-call(bf16[32,2048]{1,0:T(8,128)(2,1)} %bitcast.11, bf16[32,512]{1,0:T(8,128)(2,1)} %bitcast.13, bf16[32,512]{1,0:T(8,128)(2,1)} %bitcast.14, bf16[32,2048]{1,0:T(8,128)(2,1)} %bitcast.12, ...), custom_call_target="tpu_custom_call" | custom-call | tf_op jit(solution)/shard_map/pallas_call | solution.py:436
  48.3 1.8 %shard_map.112 = (bf16[32,2048]{1,0:T(8,128)(2,1)}, bf16[32,512]{1,0:T(8,128)(2,1)}, bf16[32,512]{1,0:T(8,128)(2,1)}, f32[32,128]{1,0:T(8,128)}) custom-call(bf16[4,32,512]{2,1,0:T(8,128)(2,1)} %get-tuple-element.13.dqr, bf16[4,32,256]{2,1,0:T(8,128)(2,1)} %get-tuple-element.14.kr, f32[32,128]{1,0:T(8,128)} %get-tuple-element.15.cos_s, ...), custom_call_target="tpu_custom_call" | custom-call | tf_op jit(solution)/shard_map/pallas_call | solution.py:461

commit v7 on v6

--- a/solution.py
+++ b/solution.py
@@ -48,8 +48,8 @@
 
 def kernel(
     q_hbm, k_hbm, v_hbm, g_hbm, x_hbm, w_hbm, p_hbm, rope_hbm,
-    dqr, kr, cos_s, sin_s, r_sum,
-    q_ref, k_ref, v_ref, g_ref, x_ref, w_ref, p_ref, rope_ref, in_sem, gate_s, kv4, qg4, kv, qg, q_s, g_s, s_s, d_s, dqt_s, pb, rb, dqs, cb,
+    dq_hbm, dk_hbm, dv_hbm, r_hbm,
+    q_ref, k_ref, v_ref, g_ref, x_ref, w_ref, p_ref, rope_ref, in_sem, out_sem, dq_out, dk_out, dv_out, r_out, dqr, kr, cos_s, sin_s, gate_s, kv4, qg4, kv, qg, q_s, g_s, s_s, d_s, dqt_s, pb, rb, dqs, cb,
     ts, tr, rz_s, rz, ry_s, ry, rx_s, rx,
     kv_ss, kv_rs, qg_ss, qg_rs, ga_ss, ga_rs, pb_ss, pb_rs, dq_ss, dq_rs, kr_ss, kr_rs,
     t_ss, t_rs, rz_ss, rz_rs, ry_ss, ry_rs, rx_ss, rx_rs,
@@ -152,15 +152,24 @@
         rows = kv.at[mate, pl.ds(part * ROWS, ROWS if part == 0 else 3 * ROWS)]
         return remote(rows, rows, ga_ss.at[0], ga_rs.at[run], mate_at(index))
 
+    def ga_whole(index):
+        rows = kv.at[mate]
+        return remote(rows, rows, ga_ss.at[0], ga_rs.at[run], mate_at(index))
+
     def ga_start(part):
         for number in reversed(range(1, SUPER)):
+            early = number >= 4
 
             @pl.when(number > run)
             def _():
-                ga_send(part, 2 * number).start()
-                ga_send(part, 2 * number + 1).start()
-
-        ga_send(part, run * 2 + 1 - par).start()
+                for index in (2 * number, 2 * number + 1):
+                    if early:
+                        ga_send(part, index).start()
+                    elif part == 1:
+                        ga_whole(index).start()
+
+        if part == 1:
+            ga_whole(run * 2 + 1 - par).start()
 
     for step in range(1, QUAD):
         kv_copy(step).start()
@@ -342,6 +351,22 @@
         kr_copy(step).start()
     kr[head] = cb[:ROWS]
 
+    back_cos = cos_s[...]
+    back_sin = sin_s[...]
+
+    def turn_back(rows):
+        return rows * back_cos - pltpu.roll(rows, HD // 2, 1) * back_sin
+
+    results = ((dq_out, dq_hbm), (dk_out, dk_hbm), (dv_out, dv_hbm), (r_out, r_hbm))
+    stores = [
+        pltpu.make_async_copy(src, dst, out_sem.at[number]) for number, (src, dst) in enumerate(results)
+    ]
+    settle(dqr.at[pl.ds(0, 3)], dq_rs.at[0])
+    for number in range(HQ):
+        cols = slice((number % GROUP) * HD, (number % GROUP + 1) * HD)
+        rows = dqr[number // GROUP, :, cols].astype(F32)
+        dq_out[:, number * HD : (number + 1) * HD] = turn_back(rows).astype(BF16)
+    stores[0].start()
     settle(ry.at[pl.ds(0, 15)], ry_rs.at[0])
     rx_s[...] = ring_sum(ry, 16).astype(BF16)
     swap.start()
@@ -366,29 +391,27 @@
 
     lax.fori_loop(run + 1, SUPER, drain_late, 0)
     lax.fori_loop(0, run, drain_early, 0)
+
     swap.wait()
-    r_sum[...] = ring_sum(rx, 2) * (1.0 / math.sqrt(4 * 2048))
-    settle(dqr.at[pl.ds(0, 3)], dq_rs.at[0])
+    r_out[...] = ring_sum(rx, 2) * (1.0 / math.sqrt(4 * 2048))
+    stores[3].start()
     settle(kr.at[pl.ds(0, 3)], kr_rs.at[0])
-    settle(kr.at[pl.ds(0, 3)], kr_ss.at[0])
-
-
-def finish(dqr, kr, cos_s, sin_s, r_sum, dq_out, dk_out, dv_out, r_out):
-    cos = cos_s[...]
-    sin = sin_s[...]
-
-    def turn_back(rows):
-        return rows * cos - pltpu.roll(rows, HD // 2, 1) * sin
-
-    for number in range(HQ):
-        cols = slice((number % GROUP) * HD, (number % GROUP + 1) * HD)
-        rows = dqr[number // GROUP, :, cols].astype(F32)
-        dq_out[:, number * HD : (number + 1) * HD] = turn_back(rows).astype(BF16)
     for number in range(KVH):
         cols = slice(number * HD, (number + 1) * HD)
         dk_out[:, cols] = turn_back(kr[number, :, :HD].astype(F32)).astype(BF16)
         dv_out[:, cols] = kr[number, :, HD:]
-    r_out[...] = r_sum[...]
+    stores[1].start()
+    stores[2].start()
+    settle(kr.at[pl.ds(0, 3)], kr_ss.at[0])
+    for store in stores:
+        store.wait()
+
+
+def finish(dq_in, dk_in, dv_in, r_in, dq_out, dk_out, dv_out, r_out):
+    dq_out[...] = dq_in[...]
+    dk_out[...] = dk_in[...]
+    dv_out[...] = dv_in[...]
+    r_out[...] = r_in[...]
 
 
 def shards(queries, keys, values, out_grad, routed_inputs, router_weight, positions):
@@ -405,6 +428,15 @@
         pltpu.VMEM((1, ROWS), jnp.int32),
         pltpu.VMEM((8, HD), F32),
         dma((8,)),
+        dma((4,)),
+        pltpu.VMEM((ROWS, HQ * HD), BF16),
+        pltpu.VMEM((ROWS, KVH * HD), BF16),
+        pltpu.VMEM((ROWS, KVH * HD), BF16),
+        pltpu.VMEM((32, 128), F32),
+        pltpu.VMEM((QUAD, ROWS, GROUP * HD), BF16),
+        pltpu.VMEM((QUAD, ROWS, 2 * HD), BF16),
+        pltpu.VMEM((ROWS, HD), F32),
+        pltpu.VMEM((ROWS, HD), F32),
         pltpu.VMEM((ROWS, HD), F32),
         pltpu.VMEM((KVH, ROWS, 2 * HD), BF16),
         pltpu.VMEM((QUAD, 2, ROWS, GROUP * HD), BF16),
@@ -433,17 +465,17 @@
         dma((1,)), dma((1,)), dma((1,)), dma((1,)),
         dma((1,)), dma((1,)), dma((1,)), dma((1,)),
     ]
-    landed = pl.pallas_call(
+    results = (
+        jax.ShapeDtypeStruct((ROWS, HQ * HD), BF16),
+        jax.ShapeDtypeStruct((ROWS, KVH * HD), BF16),
+        jax.ShapeDtypeStruct((ROWS, KVH * HD), BF16),
+        jax.ShapeDtypeStruct((32, 128), F32),
+    )
+    held = pl.pallas_call(
         kernel,
-        out_shape=(
-            jax.ShapeDtypeStruct((QUAD, ROWS, GROUP * HD), BF16),
-            jax.ShapeDtypeStruct((QUAD, ROWS, 2 * HD), BF16),
-            jax.ShapeDtypeStruct((ROWS, HD), F32),
-            jax.ShapeDtypeStruct((ROWS, HD), F32),
-            jax.ShapeDtypeStruct((32, 128), F32),
-        ),
+        out_shape=results,
         in_specs=[hbm] * 8,
-        out_specs=(vmem,) * 5,
+        out_specs=(hbm,) * 4,
         scratch_shapes=scratch,
         compiler_params=pltpu.CompilerParams(
             collective_id=0, has_side_effects=True, vmem_limit_bytes=63 * 1024 * 1024
@@ -460,15 +492,10 @@
     )
     query_grad, key_grad, value_grad, router = pl.pallas_call(
         finish,
-        out_shape=(
-            jax.ShapeDtypeStruct((ROWS, HQ * HD), BF16),
-            jax.ShapeDtypeStruct((ROWS, KVH * HD), BF16),
-            jax.ShapeDtypeStruct((ROWS, KVH * HD), BF16),
-            jax.ShapeDtypeStruct((32, 128), F32),
-        ),
-        in_specs=[vmem] * 5,
+        out_shape=results,
+        in_specs=[vmem] * 4,
         out_specs=(vmem,) * 4,
-    )(*landed)
+    )(*held)
     return (query_grad[None], key_grad[None], value_grad[None], router.reshape(-1))
 
 

time: 50.8 us -> 50 us (0.984); the launches traced: 50 us -> 49.9 us
  no operation moved by 1% of the time
where the time goes in v7:
time: 50 us; the launch traced here: 49.9 us
  Pallas kernels  49.2 us (98%)
  between operations  0.64 us (1%)
    pallas_call x1, Pallas kernels, shards(): pl.pallas_call(kernel, out_shape=results, in_specs=[hbm] * 8, out_specs=(...  47.6 us
    pallas_call x1, Pallas kernels, shards(): pl.pallas_call(finish, out_shape=results, in_specs=[vmem] * 4, out_specs=...  1.61 us

profile of v7, /device:TPU:1, one launch (start us, length us, event | category | flops | bytes accessed | tf_op | source)
XLA Modules:
  0.0 49.9 jit_solution(5514860785678710224)
XLA Ops:
  0.6 47.6 %shard_map.111 = (bf16[32,2048]{1,0:T(8,128)(2,1)}, bf16[32,512]{1,0:T(8,128)(2,1)}, bf16[32,512]{1,0:T(8,128)(2,1)}, f32[32,128]{1,0:T(8,128)}) custom-call(bf16[32,2048]{1,0:T(8,128)(2,1)} %bitcast.11, bf16[32,512]{1,0:T(8,128)(2,1)} %bitcast.13, bf16[32,512]{1,0:T(8,128)(2,1)} %bitcast.14, bf16[32,2048]{1,0:T(8,128)(2,1)} %bitcast.12, ...), custom_call_target="tpu_custom_call" | custom-call | tf_op jit(solution)/shard_map/pallas_call | solution.py:474
  48.3 1.6 %shard_map.112 = (bf16[32,2048]{1,0:T(8,128)(2,1)}, bf16[32,512]{1,0:T(8,128)(2,1)}, bf16[32,512]{1,0:T(8,128)(2,1)}, f32[32,128]{1,0:T(8,128)}) custom-call(bf16[32,2048]{1,0:T(8,128)(2,1)} %get-tuple-element.12.dq_in, bf16[32,512]{1,0:T(8,128)(2,1)} %get-tuple-element.13.dk_in, bf16[32,512]{1,0:T(8,128)(2,1)} %get-tuple-element.14.dv_in, ...), custom_call_target="tpu_custom_call" | custom-call | tf_op jit(solution)/shard_map/pallas_call | solution.py:493
